TPU v7x, 256 devices: a whole 4x4x8 slice. The times are simulated.
256 devices in a mesh: blk: 64 (over x, z, core), crs: 4 (over y).
Axes of the slice: x: 4, y: 4, z: 8, core: 2. Of those that a mesh axis runs over, the one named last changes fastest.
Arguments:
- positions: float32 [3, 1024, 32, 128], P(None, 'blk', 'crs'), may hold values from 0 to 1
- pressure_start: float32 [1024, 32, 128], P('blk', 'crs'), may hold values from 0 to 2
- source: float32 [1024, 32, 128], P('blk', 'crs'), may hold values from 0.2 to 2
- resist: float32 [1024, 32, 128], P('blk', 'crs'), may hold values from 0.02 to 0.2
- neighbour_tiles: int32 [1024, 32, 6], P('blk', 'crs'), may hold values from 0 to 179, as said below
- pair_owner: int32 [524288, 1], P(('blk', 'crs')), may hold values from 0 to 63; in each aligned block of 2048 rows (0 to 2047, 2048 to 4095, ...) at most 64 rows name the same one
- pair_fluid: int32 [524288], P(('blk', 'crs')), may hold values from 0 to 16383
- pair_grain: int32 [524288], P(('blk', 'crs')), may hold values from 0 to 1023
- pair_normal: float32 [3, 524288], P(None, ('blk', 'crs')), may hold values from -6 to 6
- grain_positions: float32 [3, 262144], P(None, ('blk', 'crs')), may hold values from 0 to 1
- grain_velocity: float32 [3, 262144], P(None, ('blk', 'crs')), may hold values from -6 to 6
- grain_mass: float32 [262144], P(('blk', 'crs')), may hold values from 0.5 to 2
- contact_tiles: int32 [2048, 4], P(('blk', 'crs')), may hold values from 0 to 7
Outputs:
- pressure: float32 [1024, 32, 128], P('blk', 'crs')
- grain_new: float32 [3, 262144], P(None, ('blk', 'crs'))
- pair_velocity: float32 [3, 524288], P(None, ('blk', 'crs'))
Inputs may be any that keep to these rules, and one draw needn't show every extreme that they name: `neighbour_tiles`: the entries of one tile are distinct; the first is the tile itself and the others are 5 of its eight neighbouring tiles in the extended grid, in some order. `pair_owner`: among the rows of one device, at most 64 name one owner, a bound that some block reaches.
All inputs are finite; a program needn't handle non-finite values.
Results may differ from a plain program's by a relative error of at most 0.0001.
Values sent between devices are 32-bit elements; how exact they have to be, the bound alone decides.
No kernel may reach another device: no remote copies, remote signals or barrier semaphores. Data moves between devices by JAX's collectives and lax.ppermute only.
A program may use at most 128 MiB of HBM per device.

v0:
```python
import math

import jax
import jax.numpy as jnp
from jax import lax
from jax.sharding import PartitionSpec as P

ITERS = 3


HIGH = lax.Precision.HIGHEST


def padded(block, sides, width):
    for axis, dim in sides:
        count = lax.axis_size(axis)
        forward = [(i, i + 1) for i in range(count - 1)]
        backward = [(target, source) for source, target in forward]
        low = lax.ppermute(
            lax.slice_in_dim(block, block.shape[dim] - width, None, axis=dim), axis, forward
        )
        high = lax.ppermute(lax.slice_in_dim(block, 0, width, axis=dim), axis, backward)
        block = jnp.concatenate([low, block, high], axis=dim)
    return block


def pair_sums(own, near_pos, near_val, scale):
    dist = jnp.zeros(
        (own.shape[1], near_pos.shape[2], own.shape[2], near_pos.shape[3]), jnp.float32
    )
    for comp in range(3):
        delta = own[comp][:, None, :, None] - near_pos[comp][:, :, None, :]
        dist = dist + delta * delta
    weight = jnp.maximum(0.0, 1.0 - dist) ** 3 * (scale / (near_pos.shape[3] * near_pos.shape[2]))
    total = jnp.sum(weight, axis=(1, 3))
    applied = jnp.einsum("gkij,cgkj->cgi", weight, near_val, precision=HIGH)
    return (total, applied)


def blocked_sums(own, near_pos, near_val, scale, group):
    count = own.shape[1]

    def one_block(index):
        start = index * group
        return pair_sums(
            lax.dynamic_slice_in_dim(own, start, group, 1),
            lax.dynamic_slice_in_dim(near_pos, start, group, 1),
            lax.dynamic_slice_in_dim(near_val, start, group, 1),
            scale,
        )

    total, applied = lax.map(one_block, jnp.arange(count // group, dtype=jnp.int32))
    return (
        total.reshape(count, -1),
        jnp.moveaxis(applied, 0, 1).reshape(near_val.shape[0], count, -1),
    )


def grain_update(coupling, grain_positions, grain_velocity, grain_mass, contact_tiles):
    count = grain_velocity.shape[1]
    tiles = count // 128
    grain_pos = grain_positions.reshape(3, tiles, 128)
    grain_vel = grain_velocity.reshape(3, tiles, 128)
    total, applied = blocked_sums(
        grain_pos, grain_pos[:, contact_tiles], grain_vel[:, contact_tiles], 4.0, math.gcd(8, tiles)
    )
    contact = applied - total[None] * grain_vel
    updated = grain_vel + 0.1 * (coupling.reshape(3, tiles, 128) + contact) / grain_mass.reshape(
        tiles, 128
    )
    return updated.reshape(3, count)


def on_device(
    positions,
    pressure_start,
    source,
    resist,
    neighbour_tiles,
    pair_owner,
    pair_fluid,
    pair_grain,
    pair_normal,
    grain_positions,
    grain_velocity,
    grain_mass,
    contact_tiles,
):
    rows_x = pressure_start.shape[0]
    rows_y = pressure_start.shape[1]
    tiles = rows_x * rows_y
    near_index = neighbour_tiles.reshape(tiles, neighbour_tiles.shape[2])
    ext_pos = padded(positions, (("blk", 1), ("crs", 2)), 1).reshape(3, -1, 128)
    near_pos = ext_pos[:, near_index]
    own = positions.reshape(3, tiles, 128)
    group = math.gcd(8, tiles)
    source_rows = source.reshape(tiles, 128)
    resist_rows = resist.reshape(tiles, 128)
    press = pressure_start
    for step in range(ITERS):
        ext_press = padded(press, (("blk", 0), ("crs", 1)), 1).reshape(1, -1, 128)
        total, applied = blocked_sums(own, near_pos, ext_press[:, near_index], 1.0, group)
        press = ((source_rows + applied[0]) / (total + resist_rows)).reshape(rows_x, rows_y, 128)
    force = press.reshape(-1)[pair_fluid][None, :] * pair_normal
    target = pair_owner[:, 0]
    owners = lax.axis_size("blk")
    grain_count = grain_velocity.shape[1]
    slot_index = target * grain_count + pair_grain
    term = jax.ops.segment_sum(force.T, slot_index, num_segments=owners * grain_count).T
    coupling = lax.psum_scatter(term, "blk", scatter_dimension=1, tiled=True)
    grain_new = grain_update(coupling, grain_positions, grain_velocity, grain_mass, contact_tiles)
    column = lax.all_gather(grain_new, "blk", axis=1, tiled=True)
    seen = column[:, slot_index]
    return (press, grain_new, seen)


def solution(mesh):
    in_specs = (
        P(None, "blk", "crs", None),
        P("blk", "crs", None),
        P("blk", "crs", None),
        P("blk", "crs", None),
        P("blk", "crs", None),
        P(("blk", "crs"), None),
        P(("blk", "crs")),
        P(("blk", "crs")),
        P(None, ("blk", "crs")),
        P(None, ("blk", "crs")),
        P(None, ("blk", "crs")),
        P(("blk", "crs")),
        P(("blk", "crs"), None),
    )
    out_specs = (P("blk", "crs", None), P(None, ("blk", "crs")), P(None, ("blk", "crs")))
    return jax.shard_map(
        on_device, mesh=mesh, in_specs=in_specs, out_specs=out_specs, check_vma=False
    )
```

profile of v0, /device:TPU:1, one launch (start us, length us, event | category | flops | bytes accessed | tf_op | source)
XLA Modules:
  0.0 869.2 jit_solution(16758055343595605163)
XLA Ops:
  7.9 4.9 collective-permute-start
  25.4 4.0 collective-permute-start.6
  31.7 4.0 collective-permute-start.2
  41.7 139.2 %while.41 = (s32[]{:T(128)}, f32[16,8,128]{2,1,0:T(8,128)S(1)}, f32[16,1,8,128]{3,2,1,0:T(8,128)S(1)}, s32[16]{0:T(128)S(1)}, f32[3,128,128]{2,1,0:T(8,128)}, /*...) while((s32[]{:T(128)}, f32[16,8,128]{2,1,0:T(8,128)S(1)}, ...), condition=%wide.region_2.3_spmd, body=%wide.region_0.2_spmd.sunk | while | flops 30669832 | bytes 442619 | solution.py:52
  46.4 3.9 fusion.114
  55.1 3.9 fusion.114
  63.8 3.9 fusion.114
  72.5 3.9 fusion.114
  81.2 3.9 fusion.114
  89.9 3.9 fusion.114
  98.6 3.9 fusion.114
  107.3 3.9 fusion.114
  116.0 3.9 fusion.114
  124.7 3.9 fusion.114
  133.4 3.9 fusion.114
  142.1 3.9 fusion.114
  150.8 3.9 fusion.114
  159.5 3.9 fusion.114
  168.2 3.9 fusion.114
  176.9 3.9 fusion.114
  182.8 3.9 collective-permute-start.8
  188.7 4.2 collective-permute-start.10
  195.3 127.3 %while.42 = (s32[]{:T(128)}, f32[16,8,128]{2,1,0:T(8,128)S(1)}, f32[16,1,8,128]{3,2,1,0:T(8,128)S(1)}, s32[16]{0:T(128)S(1)}, f32[3,128,128]{2,1,0:T(8,128)}, /*...) while((s32[]{:T(128)}, f32[16,8,128]{2,1,0:T(8,128)S(1)}, ...), condition=%wide.region_5.6_spmd, body=%wide.region_3.5_spmd.sunk | while | flops 30669832 | bytes 442619 | solution.py:52
  199.3 3.9 fusion.118
  207.3 3.9 fusion.118
  215.2 3.9 fusion.118
  223.2 3.9 fusion.118
  231.1 3.9 fusion.118
  239.1 3.9 fusion.118
  247.1 3.9 fusion.118
  255.0 3.9 fusion.118
  263.0 3.9 fusion.118
  270.9 3.9 fusion.118
  278.9 3.9 fusion.118
  286.8 3.9 fusion.118
  294.8 3.9 fusion.118
  302.7 3.9 fusion.118
  310.7 3.9 fusion.118
  318.7 3.9 fusion.118
  324.5 5.3 collective-permute-start.12
  331.9 4.8 collective-permute-start.14
  339.0 127.2 %while.43 = (s32[]{:T(128)}, f32[16,8,128]{2,1,0:T(8,128)S(1)}, f32[16,1,8,128]{3,2,1,0:T(8,128)S(1)}, s32[16]{0:T(128)S(1)}, f32[3,128,128]{2,1,0:T(8,128)}, /*...) while((s32[]{:T(128)}, f32[16,8,128]{2,1,0:T(8,128)S(1)}, ...), condition=%wide.region_8.9_spmd, body=%wide.region_6.8_spmd.sunk | while | flops 30669832 | bytes 442619 | solution.py:52
  343.0 3.9 fusion.122
  351.0 3.9 fusion.122
  358.9 3.9 fusion.122
  366.9 3.9 fusion.122
  374.8 3.9 fusion.122
  382.8 3.9 fusion.122
  390.7 3.9 fusion.122
  398.7 3.9 fusion.122
  406.6 3.9 fusion.122
  414.6 3.9 fusion.122
  422.6 3.9 fusion.122
  430.5 3.9 fusion.122
  438.5 3.9 fusion.122
  446.4 3.9 fusion.122
  454.4 3.9 fusion.122
  462.3 3.9 fusion.122
  466.3 11.8 %gather_fusion.4 = f32[2048]{0:T(1024)S(1)} fusion(f32[16384]{0:T(1024)S(1)} %bitcast_divide_fusion, s32[2048]{0:T(1024)S(1)} %get-tuple-element.240), kind=kCustom, calls=%fused_computation.4 | custom fusion | bytes 24576 | tf_op jit(solution)/shard_map/gather | solution.py:104
  478.5 24.6 %scatter_custom_fusion = f32[65536,3]{1,0:T(8,128)} fusion(s32[2048]{0:T(1024)S(1)} %get-tuple-element.199, f32[2048,3]{1,0:T(8,128)S(1)} %copy.61, f32[]{:T(128)} %constant.71.clone.1), kind=kCustom, calls=%fused_computation.87 | custom fusion | flops 6144 | bytes 786436 | tf_op jit(solution)/shard_map/scatter-add | solution.py:109
  507.3 264.5 %reduce-scatter.4.cloned.1.call-done = f32[1024,3]{1,0:T(8,128)} async-done(((f32[65536,3]{1,0:T(8,128)}), f32[1024,3]{1,0:T(8,128)}) %reduce-scatter.4.cloned.1.call-update) | async-done | bytes 12304
  775.9 53.6 %all_gather.3 = f32[3,65536]{1,0:T(4,128)S(1)} all-gather(f32[3,1024]{1,0:T(4,128)S(1)} %fusion.72), channel_id=1, replica_groups=mesh['blk'=64,'crs'=4] {'blk'}, dimensions={1}, use_global_device_ids=true | all-gather | bytes 798720 | tf_op jit(solution)/shard_map/all_gather | solution.py:112
  829.5 15.9 %copy.64 = f32[3,65536]{0,1:T(8,128)} copy(f32[3,65536]{1,0:T(4,128)S(1)} %all_gather.3) | data formatting | bytes 1572864 | tf_op jit(solution)/shard_map/all_gather | solution.py:112
  845.4 16.0 %gather_fusion.7 = f32[2048,3]{1,0:T(8,128)S(1)} fusion(f32[3,65536]{0,1:T(8,128)} %copy.64, s32[2048]{0:T(1024)S(1)} %get-tuple-element.198), kind=kCustom, calls=%fused_computation.7 | custom fusion | bytes 57344 | tf_op jit(solution)/shard_map/gather | solution.py:113
  (452 shorter events, 216.7 us)
Async XLA Ops:
  7.2 764.7 %reduce-scatter.4.cloned.1.call-start = ((), (), s32[]{:S(2)}) async-start(), calls=%async_computation.1 | async-start | bytes 34078720
  7.9 21.4 %collective-permute-start = (f32[3,1,8,128]{3,2,1,0:T(8,128)S(1)}, f32[3,1,8,128]{3,2,1,0:T(8,128)S(1)}, u32[]{:S(2)}, u32[]{:S(2)}) collective-permute-start(f32[3,1,8,128]{3,2,1,0:T(8,128)S(1)} %get-tuple-element.221), channel_id=1, source_target_pairs={{0,4},{4,8},{8,12},{12,16},{16,20},{20,24},{24,28},{28,32},{32,36}... | collective-permute-start | bytes 36872 | tf_op jit(solution)/shard_map/ppermute | solution.py:19
  12.9 17.5 %collective-permute-start.1 = (f32[3,1,8,128]{3,2,1,0:T(8,128)S(1)}, f32[3,1,8,128]{3,2,1,0:T(8,128)S(1)}, u32[]{:S(2)}, u32[]{:S(2)}) collective-permute-start(f32[3,1,8,128]{3,2,1,0:T(8,128)S(1)} %get-tuple-element.220), channel_id=1, source_target_pairs={{4,0},{8,4},{12,8},{16,12},{20,16},{24,20},{28,24},{32,28},{36,32}... | collective-permute-start | bytes 36872 | tf_op jit(solution)/shard_map/ppermute | solution.py:22
  15.5 6.8 collective-permute-start.4
  19.1 4.9 collective-permute-start.5
  24.1 11.6 %collective-permute-start.7 = (f32[18,1,128]{2,1,0:T(1,128)S(1)}, f32[18,1,128]{2,1,0:T(1,128)S(1)}, u32[]{:S(2)}, u32[]{:S(2)}) collective-permute-start(f32[18,1,128]{2,1,0:T(1,128)S(1)} %get-tuple-element.227), channel_id=1, source_target_pairs={{1,0},{2,1},{3,2},{5,4},{6,5},{7,6},{9,8},{10,9},{11,10},{13,12},{... | collective-permute-start | bytes 27656 | tf_op jit(solution)/shard_map/ppermute | solution.py:22
  25.4 10.3 %collective-permute-start.6 = (f32[18,1,128]{2,1,0:T(1,128)S(1)}, f32[18,1,128]{2,1,0:T(1,128)S(1)}, u32[]{:S(2)}, u32[]{:S(2)}) collective-permute-start(f32[18,1,128]{2,1,0:T(1,128)S(1)} %get-tuple-element.226), channel_id=1, source_target_pairs={{0,1},{1,2},{2,3},{4,5},{5,6},{6,7},{8,9},{9,10},{10,11},{12,13},{... | collective-permute-start | bytes 27656 | tf_op jit(solution)/shard_map/ppermute | solution.py:19
  30.4 7.8 collective-permute-start.3
  31.7 6.5 collective-permute-start.2
  41.6 139.2 %copy-start = (f32[16,8,128]{2,1,0:T(8,128)S(1)}, f32[16,8,128]{2,1,0:T(8,128)}, u32[]{:S(2)}) copy-start(f32[16,8,128]{2,1,0:T(8,128)} %param.21) | copy-start | bytes 196612
  41.6 139.2 %copy-start.1 = (f32[16,8,128]{2,1,0:T(8,128)S(1)}, f32[16,8,128]{2,1,0:T(8,128)}, u32[]{:S(2)}) copy-start(f32[16,8,128]{2,1,0:T(8,128)} %param.22) | copy-start | bytes 196612
  41.6 151.3 %copy-start.6 = (s32[2048,1]{0,1:T(1,128)S(1)}, s32[2048,1]{0,1:T(1,128)}, u32[]{:S(2)}) copy-start(s32[2048,1]{0,1:T(1,128)} %param.24) | copy-start | bytes 24580
  180.9 5.8 collective-permute-start.9
  182.8 4.6 collective-permute-start.8
  187.4 5.5 collective-permute-start.11
  188.7 4.8 collective-permute-start.10
  195.3 141.4 %copy-start.7 = (s32[2048]{0:T(1024)S(1)}, s32[2048]{0:T(1024)}, u32[]{:S(2)}) copy-start(s32[2048]{0:T(1024)} %param.26) | copy-start | bytes 24580
  195.3 141.4 %copy-start.8 = (s32[2048]{0:T(1024)S(1)}, s32[2048]{0:T(1024)}, u32[]{:S(2)}) copy-start(s32[2048]{0:T(1024)} %param.25) | copy-start | bytes 24580
  322.6 7.3 collective-permute-start.13
  324.5 6.1 collective-permute-start.12
  330.6 6.1 collective-permute-start.15
  331.9 5.3 collective-permute-start.14
  466.3 11.8 %copy-start.4 = (f32[3,2048]{1,0:T(4,128)S(1)}, f32[3,2048]{1,0:T(4,128)}, u32[]{:S(2)}) copy-start(f32[3,2048]{1,0:T(4,128)} %param.27) | copy-start | bytes 73732
  503.1 0.7 copy-start.9
  503.1 0.9 copy-start.3
  503.1 1.5 copy-start.2
  503.1 269.9 %copy-start.10 = (f32[1024]{0:T(1024)S(1)}, f32[1024]{0:T(1024)}, u32[]{:S(2)}) copy-start(f32[1024]{0:T(1024)} %param.30) | copy-start | bytes 12292
  775.9 69.6 %copy-start.5 = (f32[3,1024]{1,0:T(4,128)}, f32[3,1024]{1,0:T(4,128)S(1)}, u32[]{:S(2)}) copy-start(f32[3,1024]{1,0:T(4,128)S(1)} %fusion.72) | copy-start | bytes 36868
Sparse Core Ops, SparseCore 0:
  503.3 268.5 reduce-scatter.3
where the time goes:
time: 873 us; the launch traced here: 869 us
  waiting for transfers between devices  268 us (31%)
  matrix products  190 us (22%)
  local copies, waits for them, and re-layouts  140 us (16%)
  other arithmetic  122 us (14%)
  blocking collectives  53.6 us (6%)
  starting transfers between devices  47.5 us (5%)
  loops' own time  33 us (4%)
  between operations  14.7 us (2%)
    unnamed x2, waiting for transfers between devices  265 us
    dot_general x49, matrix products, pair_sums(): applied = jnp.einsum('gkij,cgkj->cgi', weight, near_val, precision=HIGH)  190 us
    reduce_sum x49, other arithmetic, pair_sums(): total = jnp.sum(weight, axis=(1, 3))  96.8 us
    all_gather x1, blocking collectives, on_device(): column = lax.all_gather(grain_new, 'blk', axis=1, tiled=True)  53.6 us
    sub x96, local copies, waits for them, and re-layouts, pair_sums(): delta = own[comp][:, None, :, None] - near_pos[comp][:, :, None, :]  35.9 us
    ppermute x8, starting transfers between devices, padded(): lax.ppermute(lax.slice_in_dim(block, block.shape[dim] - width, None, axis...  34.6 us
    another operation x3, loops' own time, blocked_sums(): lax.map(one_block, jnp.arange(count // group, dtype=jnp.int32))  33 us
    dynamic_slice x48, local copies, waits for them, and re-layouts, blocked_sums(): lax.map(one_block, jnp.arange(count // group, dtype=jnp.int32))  28.8 us
  transfers between devices with their start and end apart: 17, of which 6 were waited for; matrix products, arithmetic and copies ran while one was open for 1% of the time, Pallas kernels for 0%

commit v1 on v0

v1 whole, which is shorter than its diff:
```python
import jax
import jax.numpy as jnp
from jax import lax
from jax.experimental import pallas as pl
from jax.experimental.pallas import tpu as pltpu
from jax.sharding import PartitionSpec as P

TX, TY, L, KN, ITERS = 16, 8, 128, 6, 3
HALO = ITERS
EX = TX + 2 * HALO
EY = 16
TILES = EX * EY
PLANES = 7
K = 32
CAP = 64
F32, BF16, I32 = jnp.float32, jnp.bfloat16, jnp.int32
NT = (((1,), (1,)), ((), ()))
NN = (((1,), (0,)), ((), ()))
TN = (((0,), (0,)), ((), ()))


def dot(a, b, dims):
    return lax.dot_general(a, b, dims, preferred_element_type=F32)


def split3(x):
    high = x.astype(BF16).astype(F32)
    rest = x - high
    mid = rest.astype(BF16).astype(F32)
    return high, mid, rest - mid


def iota(shape, dim):
    return lax.broadcasted_iota(I32, shape, dim)


def distance_rows(xyz):
    left, right = [], []
    for comp in xyz:
        h, m, l = split3(comp)
        left += [2 * h, 2 * m, 2 * h, 2 * l, 2 * h, 2 * m]
        right += [h, h, m, h, l, m]
    norm = xyz[0] * xyz[0] + xyz[1] * xyz[1] + xyz[2] * xyz[2]
    one = jnp.ones_like(norm)
    left += list(split3(1.0 - norm)) + [one] * 3
    right += [one] * 3 + list(split3(-norm))
    return left, right


def store_rows(stage, rows, first, count):
    for k, row in enumerate(rows):
        stage[pl.ds(first * K + k, count, stride=K), :] = row


def cube(t):
    w = jnp.maximum(t, 0.0)
    return w * w * w


def column_sum(acc):
    return jnp.sum(acc.T, axis=0, keepdims=True)


def prep_kernel(contact_ref, owner_ref, pos_ref, vel_ref, mass_ref, rank_ref, base_ref, gain_ref, stage_a, stage_b):
    owner = owner_ref[...]
    upper = (iota((256, 256), 0) < iota((256, 256), 1)).astype(BF16)
    every = jnp.ones((256, 256), BF16)
    carry = jnp.zeros((64, 256), F32)
    for q in range(0, owner.shape[1], 256):
        named = iota((64, 256), 0) == owner[:, q : q + 256]
        hot = named.astype(F32).astype(BF16)
        before = dot(hot, upper, NN) + carry
        rank_ref[:, q : q + 256] = jnp.sum(jnp.where(named, before, 0.0), axis=0, keepdims=True).astype(I32)
        carry = carry + dot(hot, every, NN)
    tiles = vel_ref.shape[1]
    stage_a[...] = jnp.zeros_like(stage_a)
    stage_b[...] = jnp.zeros_like(stage_b)
    left, right = distance_rows([pos_ref[c] for c in range(3)])
    store_rows(stage_a, left, 0, tiles)
    store_rows(stage_b, right, 0, tiles)
    gain = 0.1 / mass_ref[...]
    gain_ref[...] = gain
    for t in range(tiles):
        a = stage_a[t * K : (t + 1) * K, :].astype(BF16)
        total = jnp.zeros((L, L), F32)
        applied = [jnp.zeros((L, L), F32) for _ in range(3)]
        for k in range(4):
            n = contact_ref[t * 4 + k]
            b = stage_b[pl.ds(pl.multiple_of(n * K, K), K), :].astype(BF16)
            w = cube(dot(a, b, TN))
            total = total + w
            for c in range(3):
                applied[c] = applied[c] + w * vel_ref[c, pl.ds(n, 1), :]
        total = column_sum(total)
        for c in range(3):
            own = vel_ref[c, t : t + 1, :]
            contact = (column_sum(applied[c]) - total * own) * (4.0 / 512)
            base_ref[c, t : t + 1, :] = own + gain[t : t + 1, :] * contact


def fluid_kernel(
    own_pos, own_press, own_src, own_res, own_dir, ylow, yhigh, xlow, xhigh, owner_ref, rank_ref, fluid_ref, grain_ref, normal_ref,
    press_ref, send_ref,
    ext, near_v, near_s, stage, left_s, right_s, num_s, deg_s, sem,
):
    blk, crs = lax.axis_index("blk"), lax.axis_index("crs")
    blks, crss = lax.axis_size("blk"), lax.axis_size("crs")
    ext[:, HALO * EY : (HALO + TX) * EY, :] = jnp.zeros((PLANES, TX * EY, L), F32)
    for x in range(HALO):
        for p in range(PLANES):
            ext[p, x * EY : (x + 1) * EY, :] = xlow[p, x]
            ext[p, (HALO + TX + x) * EY : (HALO + TX + x + 1) * EY, :] = xhigh[p, x]
    for x in range(TX):
        r = (HALO + x) * EY
        for p, plane in enumerate((own_pos.at[0], own_pos.at[1], own_pos.at[2], own_press, own_src, own_res, own_dir)):
            ext[p, r : r + TY, :] = plane[x]
            ext[p, r + TY : r + TY + HALO, :] = yhigh[p, x]
            ext[p, r + EY - HALO : r + EY, :] = ylow[p, x]
    stage[...] = jnp.zeros_like(stage)

    def build(ex, _):
        r = pl.multiple_of(ex * EY, EY)
        way = ext[6, pl.ds(r, EY), :].astype(I32)
        dx = lax.shift_right_logical(way * 11, 5)
        dy = way - 3 * dx - 1
        near_v[pl.ds(r, EY), :] = (ex + dx - 1) * EY + ((iota((EY, L), 0) + dy) & (EY - 1))
        left, right = distance_rows([ext[c, pl.ds(r, EY), :] for c in range(3)])
        for rows, target in ((left, left_s), (right, right_s)):
            for half in range(0, EY, 8):
                store_rows(stage, [row[half : half + 8] for row in rows], half, 8)
            target[pl.ds(pl.multiple_of(r * K, EY * K), EY * K), :] = stage[...].astype(BF16)
        return 0

    lax.fori_loop(0, EX, build, 0)
    copy = pltpu.make_async_copy(near_v, near_s, sem)
    copy.start()
    copy.wait()

    def one_tile(t, with_deg):
        a = left_s[pl.ds(pl.multiple_of(t * K, K), K), :]
        acc = jnp.zeros((L, L), F32)
        tot = jnp.zeros((L, L), F32)
        for k in range(0, KN, 2):
            n = [near_s[t, k + e] for e in range(2)]
            b = jnp.concatenate([right_s[pl.ds(pl.multiple_of(m * K, K), K), :] for m in n], axis=1)
            w = cube(dot(a, b, TN))
            for e in range(2):
                part = w[:, e * L : (e + 1) * L]
                acc = acc + part * ext[3, pl.ds(n[e], 1), :]
                if with_deg:
                    tot = tot + part
        num_s[pl.ds(t, 1), :] = column_sum(acc)
        if with_deg:
            deg_s[pl.ds(t, 1), :] = column_sum(tot)

    for step in range(ITERS):
        ring = ITERS - 1 - step
        pairs = (TY + 2 * ring) // 2

        def row(x, _):
            def two(j, _):
                for e in range(2):
                    y = 2 * j + e + EY - ring
                    one_tile(x * EY + (y & (EY - 1)), step == 0)
                return 0

            return lax.fori_loop(0, pairs, two, 0)

        lax.fori_loop(HALO - ring, HALO + TX + ring, row, 0)

        def divide(x, _):
            r = pl.multiple_of(x * EY, EY)
            rows = pl.ds(r, EY)
            y = iota((EY, L), 0)
            y = jnp.where(y >= EY - HALO, y - EY, y)
            gy = y + crs * TY
            gx = x - HALO + blk * TX
            inside = (gy >= 0) & (gy < crss * TY) & (gx >= 0) & (gx < blks * TX)
            scale = 1.0 / (KN * L)
            new = (ext[4, rows, :] + num_s[rows, :] * scale) / (deg_s[rows, :] * scale + ext[5, rows, :])
            ext[3, rows, :] = jnp.where(inside, new, 0.0)
            return 0

        lax.fori_loop(HALO - ring, HALO + TX + ring, divide, 0)
    for x in range(TX):
        press_ref[x] = ext[3, (HALO + x) * EY : (HALO + x) * EY + TY, :]
    press = press_ref[...].reshape(TX * TY, L)
    parts = jnp.concatenate([s.astype(BF16) for s in split3(press)], axis=1)
    total01 = jnp.zeros((64, L), F32)
    total23 = jnp.zeros((64, L), F32)
    chunk = 512
    for q in range(0, owner_ref.shape[1], chunk):
        cols = slice(q, q + chunk)
        fluid = fluid_ref[:, cols]
        lane = (iota((L, chunk), 0) == (fluid & (L - 1))).astype(F32).astype(BF16)
        found = dot(parts, jnp.concatenate([lane] * 3, axis=0), NN)
        tile = iota((TX * TY, chunk), 0) == lax.shift_right_logical(fluid, 7)
        at = jnp.sum(jnp.where(tile, found, 0.0), axis=0, keepdims=True)
        owned = iota((64, chunk), 0) == owner_ref[:, cols]
        slot = iota((L, chunk), 0)
        rank = rank_ref[:, cols]
        low = (slot == rank).astype(F32).astype(BF16)
        high = (slot == rank + CAP).astype(F32).astype(BF16)
        rows = [at * normal_ref[c : c + 1, cols] for c in range(3)] + [grain_ref[:, cols].astype(F32)]

        def spread(pair):
            out = jnp.zeros((64, L), F32)
            for value, hot in zip(pair, (low, high)):
                for part in split3(value):
                    out = out + dot(jnp.where(owned, part, 0.0).astype(BF16), hot, NT)
            return out

        total01 = total01 + spread(rows[:2])
        total23 = total23 + spread(rows[2:])
    send_ref[:, :L] = total01
    send_ref[:, L:] = total23


def grain_kernel(got_ref, base_ref, gain_ref, new_ref, back_ref):
    count = got_ref.shape[1]
    grain = got_ref[3:4, :].astype(I32)
    tile = iota((8, count), 0) == lax.shift_right_logical(grain, 7)
    lane = (iota((L, count), 0) == (grain & (L - 1))).astype(F32).astype(BF16)
    rows = []
    for c in range(3):
        for part in split3(got_ref[c : c + 1, :]):
            rows.append(jnp.where(tile, part, 0.0))
    summed = dot(jnp.concatenate(rows, axis=0).astype(BF16), lane, NT)
    new = []
    for c in range(3):
        coupling = summed[c * 24 : c * 24 + 8] + summed[c * 24 + 8 : c * 24 + 16] + summed[c * 24 + 16 : c * 24 + 24]
        new.append(base_ref[c] + gain_ref[...] * coupling)
        for g in range(8):
            new_ref[c : c + 1, g * L : (g + 1) * L] = new[c][g : g + 1]
    parts = jnp.concatenate([s.astype(BF16) for s in split3(jnp.concatenate(new, axis=0))], axis=1)
    found = dot(parts, jnp.concatenate([lane] * 3, axis=0), NN)
    for c in range(3):
        back_ref[c : c + 1, :] = jnp.sum(jnp.where(tile, found[c * 8 : c * 8 + 8], 0.0), axis=0, keepdims=True)


def pick_kernel(got_ref, owner_ref, rank_ref, out_ref):
    blocks = jnp.concatenate([got_ref[:, c * CAP : (c + 1) * CAP] for c in range(3)], axis=0)
    parts = [s.astype(BF16) for s in split3(blocks)]
    chunk = 512
    for q in range(0, owner_ref.shape[1], chunk):
        cols = slice(q, q + chunk)
        slot = (iota((CAP, chunk), 0) == rank_ref[:, cols]).astype(F32).astype(BF16)
        found = dot(parts[0], slot, NN) + dot(parts[1], slot, NN) + dot(parts[2], slot, NN)
        owned = iota((64, chunk), 0) == owner_ref[:, cols]
        for c in range(3):
            out_ref[c : c + 1, cols] = jnp.sum(jnp.where(owned, found[c * 64 : (c + 1) * 64], 0.0), axis=0, keepdims=True)


VMEM = pl.BlockSpec(memory_space=pltpu.VMEM)
SMEM = pl.BlockSpec(memory_space=pltpu.SMEM)


def shape(*dims, dtype=F32):
    return jax.ShapeDtypeStruct(dims, dtype)


def cost(flops, size):
    return pl.CostEstimate(flops=flops, bytes_accessed=size, transcendentals=0)


def shifts(axis):
    count = lax.axis_size(axis)
    forward = [(i, i + 1) for i in range(count - 1)]
    return forward, [(b, a) for a, b in forward]


def on_device(positions, pressure_start, source, resist, neighbour_tiles, pair_owner, pair_fluid, pair_grain, pair_normal,
              grain_positions, grain_velocity, grain_mass, contact_tiles):
    pairs = pair_fluid.shape[0]
    owner = pair_owner.reshape(1, pairs)
    fluid = pair_fluid.reshape(1, pairs)
    grain = pair_grain.reshape(1, pairs)
    here_x = jnp.arange(TX, dtype=I32)[:, None, None]
    here_y = jnp.arange(TY, dtype=I32)[None, :, None]
    way = (neighbour_tiles // (TY + 2) - here_x) * 3 + neighbour_tiles % (TY + 2) - here_y
    way = jnp.pad(way.astype(F32), ((0, 0), (0, 0), (0, L - KN)))

    def planes(xs, ys):
        return jnp.concatenate(
            [positions[:, xs, ys], pressure_start[None, xs, ys], source[None, xs, ys], resist[None, xs, ys], way[None, xs, ys]], axis=0
        )

    every, first, last = slice(None), slice(0, HALO), slice(-HALO, None)
    forward, backward = shifts("crs")
    ylow = lax.ppermute(planes(every, last), "crs", forward)
    yhigh = lax.ppermute(planes(every, first), "crs", backward)
    gap = jnp.zeros((PLANES, HALO, EY - TY - 2 * HALO, L), F32)

    def wide(xs):
        return jnp.concatenate([planes(xs, every), yhigh[:, xs], gap, ylow[:, xs]], axis=2)

    forward, backward = shifts("blk")
    xlow = lax.ppermute(wide(last), "blk", forward)
    xhigh = lax.ppermute(wide(first), "blk", backward)

    grain_tiles = grain_mass.shape[0] // L
    rank, base, gain = pl.pallas_call(
        prep_kernel,
        out_shape=(shape(1, pairs, dtype=I32), shape(3, grain_tiles, L), shape(grain_tiles, L)),
        in_specs=[SMEM] + [VMEM] * 4,
        out_specs=(VMEM,) * 3,
        scratch_shapes=[pltpu.VMEM((grain_tiles * K, L), F32)] * 2,
        compiler_params=pltpu.CompilerParams(vmem_limit_bytes=32 << 20),
        cost_estimate=cost(10**9, 10**6),
        name="prep",
    )(contact_tiles.reshape(-1), owner, grain_positions.reshape(3, grain_tiles, L), grain_velocity.reshape(3, grain_tiles, L), grain_mass.reshape(grain_tiles, L))

    press, send = pl.pallas_call(
        fluid_kernel,
        out_shape=(shape(TX, TY, L), shape(64, 4 * CAP)),
        in_specs=[VMEM] * 14,
        out_specs=(VMEM,) * 2,
        scratch_shapes=[
            pltpu.VMEM((PLANES, TILES, L), F32),
            pltpu.VMEM((TILES, L), I32),
            pltpu.SMEM((TILES, L), I32),
            pltpu.VMEM((EY * K, L), F32),
            pltpu.VMEM((TILES * K, L), BF16),
            pltpu.VMEM((TILES * K, L), BF16),
            pltpu.VMEM((TILES, L), F32),
            pltpu.VMEM((TILES, L), F32),
            pltpu.SemaphoreType.DMA,
        ],
        compiler_params=pltpu.CompilerParams(vmem_limit_bytes=32 << 20),
        cost_estimate=cost(10**10, 10**7),
        name="fluid",
    )(positions, pressure_start, source, resist, way, ylow, yhigh, xlow, xhigh, owner, rank, fluid, grain, pair_normal)

    got = lax.all_to_all(send, "blk", 0, 0, tiled=True)
    got = got.reshape(64, 4, CAP).swapaxes(0, 1).reshape(4, 64 * CAP)
    grain_new, back = pl.pallas_call(
        grain_kernel,
        out_shape=(shape(3, grain_tiles * L), shape(3, 64 * CAP)),
        in_specs=[VMEM] * 3,
        out_specs=(VMEM,) * 2,
        compiler_params=pltpu.CompilerParams(vmem_limit_bytes=32 << 20),
        cost_estimate=cost(10**9, 10**6),
        name="grain",
    )(got, base, gain)
    back = back.reshape(3, 64, CAP).swapaxes(0, 1).reshape(64, 3 * CAP)
    seen = lax.all_to_all(back, "blk", 0, 0, tiled=True)
    seen = pl.pallas_call(
        pick_kernel,
        out_shape=shape(3, pairs),
        in_specs=[VMEM] * 3,
        out_specs=VMEM,
        compiler_params=pltpu.CompilerParams(vmem_limit_bytes=32 << 20),
        cost_estimate=cost(10**9, 10**6),
        name="pick",
    )(seen, owner, rank)
    return press, grain_new, seen


def solution(mesh):
    in_specs = (
        P(None, "blk", "crs", None),
        P("blk", "crs", None),
        P("blk", "crs", None),
        P("blk", "crs", None),
        P("blk", "crs", None),
        P(("blk", "crs"), None),
        P(("blk", "crs")),
        P(("blk", "crs")),
        P(None, ("blk", "crs")),
        P(None, ("blk", "crs")),
        P(None, ("blk", "crs")),
        P(("blk", "crs")),
        P(("blk", "crs"), None),
    )
    out_specs = (P("blk", "crs", None), P(None, ("blk", "crs")), P(None, ("blk", "crs")))
    return jax.shard_map(on_device, mesh=mesh, in_specs=in_specs, out_specs=out_specs, check_vma=False)
```

time: 873 us -> 189 us (0.22)
  waiting for transfers between devices: 268 us -> 4.02 us
  matrix products: 190 us -> 0 us
  local copies, waits for them, and re-layouts: 140 us -> 5.16 us
  Pallas kernels: 0 us -> 128 us
  other arithmetic: 122 us -> 0.33 us
  starting transfers between devices: 47.5 us -> 14.3 us
  loops' own time: 33 us -> 0 us
  blocking collectives: 53.6 us -> 34.9 us
  between operations: 14.7 us -> 0.88 us
    unnamed x2 -> x0, waiting for transfers between devices: 265 us -> none
    dot_general x49 -> x0, matrix products: 190 us -> none  [pair_sums(): applied = jnp.einsum('gkij,cgkj->cgi', weight, near_val, precision=HIGH)]
    pallas_call x0 -> x4, Pallas kernels: none -> 128 us  [the longest x1 123 us: on_device(): pl.pallas_call(fluid_kernel, out_shape=(shape(TX, TY, L), shape(64, 4 * C...]
    reduce_sum x49 -> x0, other arithmetic: 96.8 us -> none  [pair_sums(): total = jnp.sum(weight, axis=(1, 3))]
    all_gather x1 -> x0, blocking collectives: 53.6 us -> none  [on_device(): column = lax.all_gather(grain_new, 'blk', axis=1, tiled=True)]
    gather x12 -> x0, local copies, waits for them, and re-layouts: 37.7 us -> none  [the longest x1 16 us: on_device(): seen = column[:, slot_index]]
    sub x96 -> x0, local copies, waits for them, and re-layouts: 35.9 us -> none  [pair_sums(): delta = own[comp][:, None, :, None] - near_pos[comp][:, :, None, :]]
    all_to_all x0 -> x2, blocking collectives: none -> 34.9 us  [the longest x1 21.3 us: on_device(): got = lax.all_to_all(send, 'blk', 0, 0, tiled=True)]
  transfers between devices with their start and end apart: 17 -> 4, of which waited for: 6 -> 3; matrix products, arithmetic and copies ran while one was open for 1% -> 0% of each run, Pallas kernels for 0% -> 1%
where the time goes in v1:
time: 189 us; the launch traced here: 188 us
  Pallas kernels  128 us (68%)
  blocking collectives  34.9 us (18%)
  starting transfers between devices  14.3 us (8%)
  local copies, waits for them, and re-layouts  5.16 us (3%)
  waiting for transfers between devices  4.02 us (2%)
    pallas_call x1, Pallas kernels, on_device(): pl.pallas_call(fluid_kernel, out_shape=(shape(TX, TY, L), shape(64, 4 * C...  123 us
    all_to_all x1, blocking collectives, on_device(): got = lax.all_to_all(send, 'blk', 0, 0, tiled=True)  21.3 us
    all_to_all x1, blocking collectives, on_device(): seen = lax.all_to_all(back, 'blk', 0, 0, tiled=True)  13.6 us
    ppermute x1, starting transfers between devices, on_device(): xlow = lax.ppermute(wide(last), 'blk', forward)  6.44 us
    ppermute x1, starting transfers between devices, on_device(): ylow = lax.ppermute(planes(every, last), 'crs', forward)  4.67 us
    unnamed x37, local copies, waits for them, and re-layouts  4.32 us
  transfers between devices with their start and end apart: 4, of which 3 were waited for; matrix products, arithmetic and copies ran while one was open for 0% of the time, Pallas kernels for 1%

profile of v1, /device:TPU:1, one launch (start us, length us, event | category | flops | bytes accessed | tf_op | source)
XLA Modules:
  0.0 187.9 jit_solution(2767518629412138220)
XLA Ops:
  0.6 0.0 copy-start.9
  0.6 1.1 slice_dynamic-update-slice_fusion
  1.7 0.0 copy-done.9
  1.7 0.1 copy.29
  1.8 0.0 copy-start.1
  1.9 0.1 fusion.4
  1.9 0.7 copy-done.1
  2.7 0.0 copy-start.2
  2.7 0.0 copy-start.3
  2.7 0.8 copy-done.2
  3.5 0.0 copy-start
  3.6 0.0 copy-done.3
  3.6 1.3 collective-permute-start.1
  4.9 4.7 %collective-permute-start = (f32[7,16,3,128]{3,2,1,0:T(4,128)S(1)}, f32[7,16,3,128]{3,2,1,0:T(4,128)S(1)}, u32[]{:S(2)}, u32[]{:S(2)}) collective-permute-start(f32[7,16,3,128]{3,2,1,0:T(4,128)S(1)} %get-tuple-element.34), channel_id=1, source_target_pairs={{0,1},{1,2},{2,3},{4,5},{5,6},{6,7},{8,9},{9,10},{10,11},{12,13},{... | collective-permute-start | bytes 516104 | tf_op jit(solution)/shard_map/ppermute | solution.py:290
  9.6 0.0 copy-done
  9.7 0.1 pad.11.clone
  9.8 1.3 collective-permute-done.1.yhigh
  11.1 1.5 collective-permute-done.ylow
  12.6 0.0 copy-start.10
  12.6 0.0 copy-start.11
  12.6 0.1 pad_maximum_fusion.1
  12.7 6.4 %collective-permute-start.2 = (f32[7,3,16,128]{3,2,1,0:T(8,128)S(1)}, f32[7,3,16,128]{3,2,1,0:T(8,128)S(1)}, u32[]{:S(2)}, u32[]{:S(2)}) collective-permute-start(f32[7,3,16,128]{3,2,1,0:T(8,128)S(1)} %get-tuple-element.42), channel_id=1, source_target_pairs={{0,4},{4,8},{8,12},{12,16},{16,20},{20,24},{24,28},{28,32},{32,36}... | collective-permute-start | bytes 516104 | tf_op jit(solution)/shard_map/ppermute | solution.py:298
  19.1 1.9 %collective-permute-start.3 = (f32[7,3,16,128]{3,2,1,0:T(8,128)S(1)}, f32[7,3,16,128]{3,2,1,0:T(8,128)S(1)}, u32[]{:S(2)}, u32[]{:S(2)}) collective-permute-start(f32[7,3,16,128]{3,2,1,0:T(8,128)S(1)} %get-tuple-element.41), channel_id=1, source_target_pairs={{4,0},{8,4},{12,8},{16,12},{20,16},{24,20},{28,24},{32,28},{36,32}... | collective-permute-start | bytes 516104 | tf_op jit(solution)/shard_map/ppermute | solution.py:299
  21.1 0.0 copy-done.10
  21.1 0.0 copy-done.11
  21.1 0.0 copy-start.12
  21.1 0.7 copy-done.12
  21.8 0.0 copy-start.7
  21.8 0.1 copy.32
  21.9 0.1 reshape.44.contact_ref
  21.9 0.0 copy-start.8
  21.9 0.5 copy-done.7
  22.5 0.2 copy-done.8
  22.6 0.0 copy-start.4
  22.6 0.0 copy-start.5
  22.6 0.0 copy-start.6
  22.6 1.9 %prep.1 = (s32[1,2048]{1,0:T(1,128)S(1)}, f32[3,8,128]{2,1,0:T(8,128)S(1)}, f32[8,128]{1,0:T(8,128)S(1)}) custom-call(s32[32]{0:T(128)S(1)} %reshape.44.contact_ref, s32[1,2048]{1,0:T(1,128)S(1)} %bitcast.56, f32[3,8,128]{2,1,0:T(8,128)S(1)} %get-tuple-element.44.pos_ref, f32[3,8,128]{2,1,0:T(8,128)S(1)} %get-tuple-element.43.vel_ref, f32[8,128]{1,0:T(8,128)S(1)} %bitcast.59), custom_call_target="tpu_custom_call" | custom-call | flops 1000000000 | bytes 1000000 | tf_op jit(solution)/shard_map/prep/pallas_call | solution.py:302
  24.6 0.0 collective-permute-done.2.xlow
  24.6 1.3 collective-permute-done.3.xhigh
  25.8 0.0 copy-done.4
  25.9 0.0 copy-done.5
  25.9 0.0 copy-done.6
  25.9 123.3 %fluid.1 = (f32[16,8,128]{2,1,0:T(8,128)}, f32[64,256]{1,0:T(8,128)S(1)}) custom-call(f32[3,16,8,128]{3,2,1,0:T(8,128)S(1)} %copy-done, f32[16,8,128]{2,1,0:T(8,128)S(1)} %copy-done.1, f32[16,8,128]{2,1,0:T(8,128)S(1)} %copy-done.2, f32[16,8,128]{2,1,0:T(8,128)S(1)} %copy-done.3, f32[16,8,128]{2,1,0:T(8,128)S(1)} %pad.4.own_dir, ...), custom_call_target="tpu_custom_call" | custom-call | flops 10000000000 | bytes 10000000 | tf_op jit(solution)/shard_map/fluid/pallas_call | solution.py:313
  149.2 0.1 copy.33
  149.3 21.3 %all_to_all.20 = f32[64,1,256]{2,1,0:T(1,128)S(1)} all-to-all(f32[64,1,256]{2,1,0:T(1,128)S(1)} %copy.33), channel_id=1, replica_groups=mesh['blk'=64,'crs'=4] {'blk'}, dimensions={0} | all-to-all | bytes 131072 | tf_op jit(solution)/shard_map/all_to_all | solution.py:334
  170.5 0.2 reduce
  170.7 0.1 reshape.50
  170.8 0.1 reshape.51.got_ref
  170.9 1.5 grain.1
  172.4 0.1 reshape.52
  172.6 0.1 copy.35
  172.6 0.1 copy.36
  172.7 13.6 %all_to_all.21 = f32[64,1,192]{2,1,0:T(1,128)S(1)} all-to-all(f32[64,1,192]{2,1,0:T(1,128)S(1)} %copy.36), channel_id=1, replica_groups=mesh['blk'=64,'crs'=4] {'blk'}, dimensions={0} | all-to-all | bytes 98304 | tf_op jit(solution)/shard_map/all_to_all | solution.py:346
  186.4 1.5 pick.1
  (16 shorter events, 0.2 us)
Async XLA Ops:
  0.6 1.1 copy-start.9
  1.8 0.8 copy-start.1
  2.7 0.8 copy-start.2
  2.7 0.9 copy-start.3
  3.5 6.1 %copy-start = (f32[3,16,8,128]{3,2,1,0:T(8,128)S(1)}, f32[3,16,8,128]{3,2,1,0:T(8,128)}, u32[]{:S(2)}) copy-start(f32[3,16,8,128]{3,2,1,0:T(8,128)} %own_pos.1) | copy-start | bytes 589828
  3.6 7.4 %collective-permute-start.1 = (f32[7,16,3,128]{3,2,1,0:T(4,128)S(1)}, f32[7,16,3,128]{3,2,1,0:T(4,128)S(1)}, u32[]{:S(2)}, u32[]{:S(2)}) collective-permute-start(f32[7,16,3,128]{3,2,1,0:T(4,128)S(1)} %get-tuple-element.33), channel_id=1, source_target_pairs={{1,0},{2,1},{3,2},{5,4},{6,5},{7,6},{9,8},{10,9},{11,10},{13,12},{... | collective-permute-start | bytes 516104 | tf_op jit(solution)/shard_map/ppermute | solution.py:291
  4.9 7.6 %collective-permute-start = (f32[7,16,3,128]{3,2,1,0:T(4,128)S(1)}, f32[7,16,3,128]{3,2,1,0:T(4,128)S(1)}, u32[]{:S(2)}, u32[]{:S(2)}) collective-permute-start(f32[7,16,3,128]{3,2,1,0:T(4,128)S(1)} %get-tuple-element.34), channel_id=1, source_target_pairs={{0,1},{1,2},{2,3},{4,5},{5,6},{6,7},{8,9},{9,10},{10,11},{12,13},{... | collective-permute-start | bytes 516104 | tf_op jit(solution)/shard_map/ppermute | solution.py:290
  12.6 8.5 %copy-start.10 = (f32[3,1024]{1,0:T(4,128)S(1)}, f32[3,1024]{1,0:T(4,128)}, u32[]{:S(2)}) copy-start(f32[3,1024]{1,0:T(4,128)} %param.23) | copy-start | bytes 36868
  12.6 8.5 %copy-start.11 = (f32[3,1024]{1,0:T(4,128)S(1)}, f32[3,1024]{1,0:T(4,128)}, u32[]{:S(2)}) copy-start(f32[3,1024]{1,0:T(4,128)} %param.22) | copy-start | bytes 36868
  12.7 11.9 %collective-permute-start.2 = (f32[7,3,16,128]{3,2,1,0:T(8,128)S(1)}, f32[7,3,16,128]{3,2,1,0:T(8,128)S(1)}, u32[]{:S(2)}, u32[]{:S(2)}) collective-permute-start(f32[7,3,16,128]{3,2,1,0:T(8,128)S(1)} %get-tuple-element.42), channel_id=1, source_target_pairs={{0,4},{4,8},{8,12},{12,16},{16,20},{20,24},{24,28},{28,32},{32,36}... | collective-permute-start | bytes 516104 | tf_op jit(solution)/shard_map/ppermute | solution.py:298
  19.1 6.7 %collective-permute-start.3 = (f32[7,3,16,128]{3,2,1,0:T(8,128)S(1)}, f32[7,3,16,128]{3,2,1,0:T(8,128)S(1)}, u32[]{:S(2)}, u32[]{:S(2)}) collective-permute-start(f32[7,3,16,128]{3,2,1,0:T(8,128)S(1)} %get-tuple-element.41), channel_id=1, source_target_pairs={{4,0},{8,4},{12,8},{16,12},{20,16},{24,20},{28,24},{32,28},{36,32}... | collective-permute-start | bytes 516104 | tf_op jit(solution)/shard_map/ppermute | solution.py:299
  21.1 0.7 copy-start.12
  21.8 0.7 copy-start.7
  21.9 0.7 copy-start.8
  22.6 3.2 %copy-start.4 = (f32[3,2048]{1,0:T(4,128)S(1)}, f32[3,2048]{1,0:T(4,128)}, u32[]{:S(2)}) copy-start(f32[3,2048]{1,0:T(4,128)} %normal_ref.1) | copy-start | bytes 73732
  22.6 3.2 %copy-start.5 = (s32[2048]{0:T(1024)S(1)}, s32[2048]{0:T(1024)}, u32[]{:S(2)}) copy-start(s32[2048]{0:T(1024)} %param.19) | copy-start | bytes 24580
  22.6 3.2 %copy-start.6 = (s32[2048]{0:T(1024)S(1)}, s32[2048]{0:T(1024)}, u32[]{:S(2)}) copy-start(s32[2048]{0:T(1024)} %param.20) | copy-start | bytes 24580

commit v2 on v1

--- a/solution.py
+++ b/solution.py
@@ -101,7 +101,7 @@
 def fluid_kernel(
     own_pos, own_press, own_src, own_res, own_dir, ylow, yhigh, xlow, xhigh, owner_ref, rank_ref, fluid_ref, grain_ref, normal_ref,
     press_ref, send_ref,
-    ext, near_v, near_s, stage, left_s, right_s, num_s, deg_s, sem,
+    ext, near_v, near_s, stage, left_s, right_s, num_s, deg_s, kept, sem,
 ):
     blk, crs = lax.axis_index("blk"), lax.axis_index("crs")
     blks, crss = lax.axis_size("blk"), lax.axis_size("crs")
@@ -136,7 +136,7 @@
     copy.start()
     copy.wait()
 
-    def one_tile(t, with_deg):
+    def one_tile(t, with_deg, slot=None):
         a = left_s[pl.ds(pl.multiple_of(t * K, K), K), :]
         acc = jnp.zeros((L, L), F32)
         tot = jnp.zeros((L, L), F32)
@@ -146,6 +146,8 @@
             w = cube(dot(a, b, TN))
             for e in range(2):
                 part = w[:, e * L : (e + 1) * L]
+                if slot is not None:
+                    kept[slot, k + e] = part
                 acc = acc + part * ext[3, pl.ds(n[e], 1), :]
                 if with_deg:
                     tot = tot + part
@@ -153,20 +155,41 @@
         if with_deg:
             deg_s[pl.ds(t, 1), :] = column_sum(tot)
 
+    def kept_tile(t, slot):
+        acc = jnp.zeros((L, L), F32)
+        for k in range(KN):
+            acc = acc + kept[slot, k] * ext[3, pl.ds(near_s[t, k], 1), :]
+        num_s[pl.ds(t, 1), :] = column_sum(acc)
+
     for step in range(ITERS):
         ring = ITERS - 1 - step
-        pairs = (TY + 2 * ring) // 2
-
-        def row(x, _):
-            def two(j, _):
-                for e in range(2):
-                    y = 2 * j + e + EY - ring
-                    one_tile(x * EY + (y & (EY - 1)), step == 0)
-                return 0
-
-            return lax.fori_loop(0, pairs, two, 0)
-
-        lax.fori_loop(HALO - ring, HALO + TX + ring, row, 0)
+
+        def outer_row(i, _):
+            x = HALO - ring + i + jnp.where(i >= ring, TX, 0)
+            for y in range(-ring, TY + ring):
+                one_tile(x * EY + y % EY, step == 0)
+            return 0
+
+        def own_row(i, _):
+            for y in range(-ring, TY + ring):
+                t = (i + HALO) * EY + y % EY
+                if y < 0 or y >= TY:
+                    one_tile(t, step == 0)
+                elif step == 0:
+                    one_tile(t, True, i * TY + y)
+                else:
+                    kept_tile(t, i * TY + y)
+            return 0
+
+        def own_rows(i, _):
+            own_row(2 * i, 0)
+            return own_row(2 * i + 1, 0)
+
+        if ring:
+            lax.fori_loop(0, 2 * ring, outer_row, 0)
+            lax.fori_loop(0, TX, own_row, 0)
+        else:
+            lax.fori_loop(0, TX // 2, own_rows, 0)
 
         def divide(x, _):
             r = pl.multiple_of(x * EY, EY)
@@ -324,9 +347,10 @@
             pltpu.VMEM((TILES * K, L), BF16),
             pltpu.VMEM((TILES, L), F32),
             pltpu.VMEM((TILES, L), F32),
+            pltpu.VMEM((TX * TY, KN, L, L), F32),
             pltpu.SemaphoreType.DMA,
         ],
-        compiler_params=pltpu.CompilerParams(vmem_limit_bytes=32 << 20),
+        compiler_params=pltpu.CompilerParams(vmem_limit_bytes=60 << 20),
         cost_estimate=cost(10**10, 10**7),
         name="fluid",
     )(positions, pressure_start, source, resist, way, ylow, yhigh, xlow, xhigh, owner, rank, fluid, grain, pair_normal)

time: 189 us -> 126 us (0.67)
  Pallas kernels: 128 us -> 61.7 us
  local copies, waits for them, and re-layouts: 5.16 us -> 10.1 us
    pallas_call x1, Pallas kernels: 123 us -> 56.8 us  [on_device(): pl.pallas_call(fluid_kernel, out_shape=(shape(TX, TY, L), shape(64, 4 * C...]
    unnamed x37 -> x43, local copies, waits for them, and re-layouts: 4.32 us -> 7.78 us
  transfers between devices with their start and end apart: 4 -> 4, of which waited for: 3 -> 3; matrix products, arithmetic and copies ran while one was open for 0% -> 1% of each run, Pallas kernels for 1% -> 2%
where the time goes in v2:
time: 126 us; the launch traced here: 125 us
  Pallas kernels  61.7 us (49%)
  blocking collectives  35.6 us (28%)
  starting transfers between devices  14.3 us (11%)
  local copies, waits for them, and re-layouts  10.1 us (8%)
  waiting for transfers between devices  2.66 us (2%)
    pallas_call x1, Pallas kernels, on_device(): pl.pallas_call(fluid_kernel, out_shape=(shape(TX, TY, L), shape(64, 4 * C...  56.8 us
    all_to_all x1, blocking collectives, on_device(): got = lax.all_to_all(send, 'blk', 0, 0, tiled=True)  21.9 us
    all_to_all x1, blocking collectives, on_device(): seen = lax.all_to_all(back, 'blk', 0, 0, tiled=True)  13.6 us
    unnamed x43, local copies, waits for them, and re-layouts  7.78 us
    ppermute x1, starting transfers between devices, on_device(): xlow = lax.ppermute(wide(last), 'blk', forward)  6.43 us
    ppermute x1, starting transfers between devices, on_device(): ylow = lax.ppermute(planes(every, last), 'crs', forward)  4.67 us
  transfers between devices with their start and end apart: 4, of which 3 were waited for; matrix products, arithmetic and copies ran while one was open for 1% of the time, Pallas kernels for 2%

profile of v2, /device:TPU:1, one launch (start us, length us, event | category | flops | bytes accessed | tf_op | source)
XLA Modules:
  0.0 125.5 jit_solution(8195214252715238990)
XLA Ops:
  0.6 0.0 copy-start.10
  0.6 1.1 slice_dynamic-update-slice_fusion
  1.7 0.0 copy-done.10
  1.7 0.1 copy.29
  1.8 0.0 copy-start.5
  1.9 0.1 fusion.4
  1.9 0.7 copy-done.5
  2.7 0.0 copy-start.6
  2.7 0.8 copy-done.6
  3.5 0.0 copy-start.7
  3.6 0.8 copy-done.7
  4.4 1.3 %collective-permute-start.1 = (f32[7,16,3,128]{3,2,1,0:T(4,128)S(1)}, f32[7,16,3,128]{3,2,1,0:T(4,128)S(1)}, u32[]{:S(2)}, u32[]{:S(2)}) collective-permute-start(f32[7,16,3,128]{3,2,1,0:T(4,128)S(1)} %get-tuple-element.33), channel_id=1, source_target_pairs={{1,0},{2,1},{3,2},{5,4},{6,5},{7,6},{9,8},{10,9},{11,10},{13,12},{... | collective-permute-start | bytes 516104 | tf_op jit(solution)/shard_map/ppermute | solution.py:314
  5.7 4.7 %collective-permute-start = (f32[7,16,3,128]{3,2,1,0:T(4,128)S(1)}, f32[7,16,3,128]{3,2,1,0:T(4,128)S(1)}, u32[]{:S(2)}, u32[]{:S(2)}) collective-permute-start(f32[7,16,3,128]{3,2,1,0:T(4,128)S(1)} %get-tuple-element.34), channel_id=1, source_target_pairs={{0,1},{1,2},{2,3},{4,5},{5,6},{6,7},{8,9},{9,10},{10,11},{12,13},{... | collective-permute-start | bytes 516104 | tf_op jit(solution)/shard_map/ppermute | solution.py:313
  10.4 0.8 constant_dynamic-update-slice_fusion.17
  11.2 0.1 pad.11.clone
  11.3 0.5 collective-permute-done.1.yhigh
  11.9 0.0 copy-start.8
  11.9 1.5 %collective-permute-done.ylow = f32[7,16,3,128]{3,2,1,0:T(4,128)S(1)} collective-permute-done((f32[7,16,3,128]{3,2,1,0:T(4,128)S(1)}, f32[7,16,3,128]{3,2,1,0:T(4,128)S(1)}, u32[]{:S(2)}, u32[]{:S(2)}) %collective-permute-start) | collective-permute-done | bytes 172064 | tf_op jit(solution)/shard_map/ppermute | solution.py:313
  13.3 0.0 copy-start.9
  13.4 0.0 copy-start.11
  13.4 0.0 copy-start.12
  13.4 0.1 pad_maximum_fusion.1
  13.5 0.0 copy-done.8
  13.5 0.5 copy-done.9
  14.0 6.4 %collective-permute-start.2 = (f32[7,3,16,128]{3,2,1,0:T(8,128)S(1)}, f32[7,3,16,128]{3,2,1,0:T(8,128)S(1)}, u32[]{:S(2)}, u32[]{:S(2)}) collective-permute-start(f32[7,3,16,128]{3,2,1,0:T(8,128)S(1)} %get-tuple-element.42), channel_id=1, source_target_pairs={{0,4},{4,8},{8,12},{12,16},{16,20},{20,24},{24,28},{28,32},{32,36}... | collective-permute-start | bytes 516104 | tf_op jit(solution)/shard_map/ppermute | solution.py:321
  20.5 1.9 %collective-permute-start.3 = (f32[7,3,16,128]{3,2,1,0:T(8,128)S(1)}, f32[7,3,16,128]{3,2,1,0:T(8,128)S(1)}, u32[]{:S(2)}, u32[]{:S(2)}) collective-permute-start(f32[7,3,16,128]{3,2,1,0:T(8,128)S(1)} %get-tuple-element.41), channel_id=1, source_target_pairs={{4,0},{8,4},{12,8},{16,12},{20,16},{24,20},{28,24},{32,28},{36,32}... | collective-permute-start | bytes 516104 | tf_op jit(solution)/shard_map/ppermute | solution.py:322
  22.4 0.0 copy-done.11
  22.4 0.0 copy-done.12
  22.4 0.0 copy-start.13
  22.4 0.6 pad.4.own_dir
  23.1 0.0 copy-done.13
  23.1 0.0 copy-start
  23.1 0.1 copy.32
  23.2 0.1 reshape.44.contact_ref
  23.3 0.0 copy-start.2
  23.3 0.5 copy-done
  23.8 0.2 copy-done.2
  24.0 1.9 %prep.1 = (s32[1,2048]{1,0:T(1,128)S(1)}, f32[3,8,128]{2,1,0:T(8,128)S(1)}, f32[8,128]{1,0:T(8,128)S(1)}) custom-call(s32[32]{0:T(128)S(1)} %reshape.44.contact_ref, s32[1,2048]{1,0:T(1,128)S(1)} %bitcast.54, f32[3,8,128]{2,1,0:T(8,128)S(1)} %get-tuple-element.44.pos_ref, f32[3,8,128]{2,1,0:T(8,128)S(1)} %get-tuple-element.43.vel_ref, f32[8,128]{1,0:T(8,128)S(1)} %bitcast.56), custom_call_target="tpu_custom_call" | custom-call | flops 1000000000 | bytes 1000000 | tf_op jit(solution)/shard_map/prep/pallas_call | solution.py:325
  25.9 0.0 copy-start.3
  25.9 0.6 copy-done.3
  26.5 0.0 collective-permute-done.2.xlow
  26.5 0.0 copy-start.14
  26.5 0.7 collective-permute-done.3.xhigh
  27.2 0.0 copy-start.15
  27.2 0.0 copy-done.14
  27.2 0.7 copy-done.15
  27.8 56.8 %fluid.1 = (f32[16,8,128]{2,1,0:T(8,128)}, f32[64,256]{1,0:T(8,128)}) custom-call(f32[3,16,8,128]{3,2,1,0:T(8,128)} %own_pos.1, f32[16,8,128]{2,1,0:T(8,128)} %own_press.1, f32[16,8,128]{2,1,0:T(8,128)} %own_src.1, f32[16,8,128]{2,1,0:T(8,128)} %own_res.1, f32[16,8,128]{2,1,0:T(8,128)} %pad.4.own_dir, f32[7,16,3,128]{3,2,1,0:T(4,128)} %copy-done.9, ...), custom_call_target="tpu_custom_call" | custom-call | flops 10000000000 | bytes 10000000 | tf_op jit(solution)/shard_map/fluid/pallas_call | solution.py:336
  84.6 0.9 copy.33
  85.5 21.9 %all_to_all.20 = f32[64,1,256]{2,1,0:T(1,128)S(1)} all-to-all(f32[64,1,256]{2,1,0:T(1,128)S(1)} %copy.33), channel_id=1, replica_groups=mesh['blk'=64,'crs'=4] {'blk'}, dimensions={0} | all-to-all | bytes 131072 | tf_op jit(solution)/shard_map/all_to_all | solution.py:358
  107.4 0.2 reduce
  107.6 0.1 reshape.50
  107.7 0.1 reshape.51.got_ref
  107.9 1.5 %grain.1 = (f32[3,1024]{1,0:T(4,128)}, f32[3,4096]{1,0:T(4,128)S(1)}) custom-call(f32[4,4096]{1,0:T(4,128)S(1)} %reshape.51.got_ref, f32[3,8,128]{2,1,0:T(8,128)S(1)} %get-tuple-element.13.base_ref, f32[8,128]{1,0:T(8,128)S(1)} %get-tuple-element.14.gain_ref), custom_call_target="tpu_custom_call" | custom-call | flops 1000000000 | bytes 1000000 | tf_op jit(solution)/shard_map/grain/pallas_call | solution.py:360
  109.4 0.1 reshape.52
  109.5 0.1 copy.35
  109.6 0.1 copy.36
  109.7 13.6 %all_to_all.21 = f32[64,1,192]{2,1,0:T(1,128)S(1)} all-to-all(f32[64,1,192]{2,1,0:T(1,128)S(1)} %copy.36), channel_id=1, replica_groups=mesh['blk'=64,'crs'=4] {'blk'}, dimensions={0} | all-to-all | bytes 98304 | tf_op jit(solution)/shard_map/all_to_all | solution.py:370
  123.3 0.0 copy-start.1
  123.3 0.0 copy-start.4
  123.3 0.7 copy-done.1
  124.0 0.0 copy-done.4
  124.0 1.5 %pick.1 = f32[3,2048]{1,0:T(4,128)} custom-call(f32[64,192]{1,0:T(8,128)S(1)} %bitcast.52, s32[1,2048]{1,0:T(1,128)S(1)} %bitcast.55, s32[1,2048]{1,0:T(1,128)S(1)} %copy-done.4), custom_call_target="tpu_custom_call" | custom-call | flops 1000000000 | bytes 1000000 | tf_op jit(solution)/shard_map/pick/pallas_call | solution.py:371
  (14 shorter events, 0.2 us)
Async XLA Ops:
  0.6 1.1 copy-start.10
  1.8 0.8 copy-start.5
  2.7 0.8 copy-start.6
  3.5 0.8 copy-start.7
  4.4 7.4 %collective-permute-start.1 = (f32[7,16,3,128]{3,2,1,0:T(4,128)S(1)}, f32[7,16,3,128]{3,2,1,0:T(4,128)S(1)}, u32[]{:S(2)}, u32[]{:S(2)}) collective-permute-start(f32[7,16,3,128]{3,2,1,0:T(4,128)S(1)} %get-tuple-element.33), channel_id=1, source_target_pairs={{1,0},{2,1},{3,2},{5,4},{6,5},{7,6},{9,8},{10,9},{11,10},{13,12},{... | collective-permute-start | bytes 516104 | tf_op jit(solution)/shard_map/ppermute | solution.py:314
  5.7 7.6 %collective-permute-start = (f32[7,16,3,128]{3,2,1,0:T(4,128)S(1)}, f32[7,16,3,128]{3,2,1,0:T(4,128)S(1)}, u32[]{:S(2)}, u32[]{:S(2)}) collective-permute-start(f32[7,16,3,128]{3,2,1,0:T(4,128)S(1)} %get-tuple-element.34), channel_id=1, source_target_pairs={{0,1},{1,2},{2,3},{4,5},{5,6},{6,7},{8,9},{9,10},{10,11},{12,13},{... | collective-permute-start | bytes 516104 | tf_op jit(solution)/shard_map/ppermute | solution.py:313
  11.9 1.6 %copy-start.8 = (f32[7,16,3,128]{3,2,1,0:T(4,128)}, f32[7,16,3,128]{3,2,1,0:T(4,128)S(1)}, u32[]{:S(2)}) copy-start(f32[7,16,3,128]{3,2,1,0:T(4,128)S(1)} %collective-permute-done.1.yhigh) | copy-start | bytes 516100
  13.3 0.7 copy-start.9
  13.4 9.0 %copy-start.11 = (f32[3,1024]{1,0:T(4,128)S(1)}, f32[3,1024]{1,0:T(4,128)}, u32[]{:S(2)}) copy-start(f32[3,1024]{1,0:T(4,128)} %param.23) | copy-start | bytes 36868
  13.4 9.0 %copy-start.12 = (f32[3,1024]{1,0:T(4,128)S(1)}, f32[3,1024]{1,0:T(4,128)}, u32[]{:S(2)}) copy-start(f32[3,1024]{1,0:T(4,128)} %param.22) | copy-start | bytes 36868
  14.0 12.5 %collective-permute-start.2 = (f32[7,3,16,128]{3,2,1,0:T(8,128)S(1)}, f32[7,3,16,128]{3,2,1,0:T(8,128)S(1)}, u32[]{:S(2)}, u32[]{:S(2)}) collective-permute-start(f32[7,3,16,128]{3,2,1,0:T(8,128)S(1)} %get-tuple-element.42), channel_id=1, source_target_pairs={{0,4},{4,8},{8,12},{12,16},{16,20},{20,24},{24,28},{28,32},{32,36}... | collective-permute-start | bytes 516104 | tf_op jit(solution)/shard_map/ppermute | solution.py:321
  20.5 6.7 %collective-permute-start.3 = (f32[7,3,16,128]{3,2,1,0:T(8,128)S(1)}, f32[7,3,16,128]{3,2,1,0:T(8,128)S(1)}, u32[]{:S(2)}, u32[]{:S(2)}) collective-permute-start(f32[7,3,16,128]{3,2,1,0:T(8,128)S(1)} %get-tuple-element.41), channel_id=1, source_target_pairs={{4,0},{8,4},{12,8},{16,12},{20,16},{24,20},{28,24},{32,28},{36,32}... | collective-permute-start | bytes 516104 | tf_op jit(solution)/shard_map/ppermute | solution.py:322
  22.4 0.7 copy-start.13
  23.1 0.7 copy-start
  23.3 0.7 copy-start.2
  25.9 0.6 copy-start.3
  26.5 0.7 copy-start.14
  27.2 0.7 copy-start.15
  123.3 0.7 copy-start.1
  123.3 0.7 copy-start.4

commit v3 on v2

--- a/solution.py
+++ b/solution.py
@@ -118,12 +118,20 @@
             ext[p, r + EY - HALO : r + EY, :] = ylow[p, x]
     stage[...] = jnp.zeros_like(stage)
 
-    def build(ex, _):
+    def find(ex, _):
         r = pl.multiple_of(ex * EY, EY)
         way = ext[6, pl.ds(r, EY), :].astype(I32)
         dx = lax.shift_right_logical(way * 11, 5)
         dy = way - 3 * dx - 1
         near_v[pl.ds(r, EY), :] = (ex + dx - 1) * EY + ((iota((EY, L), 0) + dy) & (EY - 1))
+        return 0
+
+    lax.fori_loop(0, EX, find, 0)
+    copy = pltpu.make_async_copy(near_v, near_s, sem)
+    copy.start()
+
+    def build(ex, _):
+        r = pl.multiple_of(ex * EY, EY)
         left, right = distance_rows([ext[c, pl.ds(r, EY), :] for c in range(3)])
         for rows, target in ((left, left_s), (right, right_s)):
             for half in range(0, EY, 8):
@@ -132,8 +140,6 @@
         return 0
 
     lax.fori_loop(0, EX, build, 0)
-    copy = pltpu.make_async_copy(near_v, near_s, sem)
-    copy.start()
     copy.wait()
 
     def one_tile(t, with_deg, slot=None):
@@ -226,17 +232,18 @@
         high = (slot == rank + CAP).astype(F32).astype(BF16)
         rows = [at * normal_ref[c : c + 1, cols] for c in range(3)] + [grain_ref[:, cols].astype(F32)]
 
-        def spread(pair):
-            out = jnp.zeros((64, L), F32)
-            for value, hot in zip(pair, (low, high)):
-                for part in split3(value):
-                    out = out + dot(jnp.where(owned, part, 0.0).astype(BF16), hot, NT)
-            return out
-
-        total01 = total01 + spread(rows[:2])
-        total23 = total23 + spread(rows[2:])
-    send_ref[:, :L] = total01
-    send_ref[:, L:] = total23
+        def spread(first, second, hot):
+            parts = split3(first) + split3(second)
+            out = dot(jnp.concatenate([jnp.where(owned, part, 0.0).astype(BF16) for part in parts], axis=0), hot, NT)
+            out = [out[i * 64 : (i + 1) * 64] for i in range(6)]
+            return out[0] + out[1] + out[2], out[3] + out[4] + out[5]
+
+        low0, low2 = spread(rows[0], rows[2], low)
+        high1, high3 = spread(rows[1], rows[3], high)
+        total01 = total01 + low0 + high1
+        total23 = total23 + low2 + high3
+    send_ref[:, 0, :] = total01
+    send_ref[:, 1, :] = total23
 
 
 def grain_kernel(got_ref, base_ref, gain_ref, new_ref, back_ref):
@@ -288,8 +295,16 @@
 
 def shifts(axis):
     count = lax.axis_size(axis)
-    forward = [(i, i + 1) for i in range(count - 1)]
+    forward = [(i, (i + 1) % count) for i in range(count)]
     return forward, [(b, a) for a, b in forward]
+
+
+def exchange(axis, up, down):
+    forward, backward = shifts(axis)
+    here = lax.axis_index(axis)
+    up = jnp.where(here == lax.axis_size(axis) - 1, 0.0, up)
+    down = jnp.where(here == 0, 0.0, down)
+    return lax.ppermute(up, axis, forward), lax.ppermute(down, axis, backward)
 
 
 def on_device(positions, pressure_start, source, resist, neighbour_tiles, pair_owner, pair_fluid, pair_grain, pair_normal,
@@ -309,17 +324,13 @@
         )
 
     every, first, last = slice(None), slice(0, HALO), slice(-HALO, None)
-    forward, backward = shifts("crs")
-    ylow = lax.ppermute(planes(every, last), "crs", forward)
-    yhigh = lax.ppermute(planes(every, first), "crs", backward)
+    ylow, yhigh = exchange("crs", planes(every, last), planes(every, first))
     gap = jnp.zeros((PLANES, HALO, EY - TY - 2 * HALO, L), F32)
 
     def wide(xs):
         return jnp.concatenate([planes(xs, every), yhigh[:, xs], gap, ylow[:, xs]], axis=2)
 
-    forward, backward = shifts("blk")
-    xlow = lax.ppermute(wide(last), "blk", forward)
-    xhigh = lax.ppermute(wide(first), "blk", backward)
+    xlow, xhigh = exchange("blk", wide(last), wide(first))
 
     grain_tiles = grain_mass.shape[0] // L
     rank, base, gain = pl.pallas_call(
@@ -335,7 +346,7 @@
 
     press, send = pl.pallas_call(
         fluid_kernel,
-        out_shape=(shape(TX, TY, L), shape(64, 4 * CAP)),
+        out_shape=(shape(TX, TY, L), shape(64, 2, L)),
         in_specs=[VMEM] * 14,
         out_specs=(VMEM,) * 2,
         scratch_shapes=[

time: 126 us -> 118 us (0.937)
  starting transfers between devices: 14.3 us -> 7.11 us
  waiting for transfers between devices: 2.66 us -> 7.11 us
  Pallas kernels: 61.7 us -> 57.5 us
    ppermute x4, starting transfers between devices: 14.3 us -> 7.11 us  [exchange(): return (lax.ppermute(up, axis, forward), lax.ppermute(down, axis, backward))]
    ppermute x4, waiting for transfers between devices: 2.66 us -> 7.11 us  [exchange(): return (lax.ppermute(up, axis, forward), lax.ppermute(down, axis, backward))]
    pallas_call x1, Pallas kernels: 56.8 us -> 52.6 us  [on_device(): pl.pallas_call(fluid_kernel, out_shape=(shape(TX, TY, L), shape(64, 2, L)...]
where the time goes in v3:
time: 118 us
  Pallas kernels  57.5 us (49%)
  blocking collectives  35.7 us (30%)
  local copies, waits for them, and re-layouts  9.2 us (8%)
  starting transfers between devices  7.11 us (6%)
  waiting for transfers between devices  7.11 us (6%)
    pallas_call x1, Pallas kernels, on_device(): pl.pallas_call(fluid_kernel, out_shape=(shape(TX, TY, L), shape(64, 2, L)...  52.6 us
    all_to_all x1, blocking collectives, on_device(): got = lax.all_to_all(send, 'blk', 0, 0, tiled=True)  22.1 us
    all_to_all x1, blocking collectives, on_device(): seen = lax.all_to_all(back, 'blk', 0, 0, tiled=True)  13.7 us
    unnamed x43, local copies, waits for them, and re-layouts  7.78 us
    ppermute x4, waiting for transfers between devices, exchange(): return (lax.ppermute(up, axis, forward), lax.ppermute(down, axis, backward))  7.11 us
    ppermute x4, starting transfers between devices, exchange(): return (lax.ppermute(up, axis, forward), lax.ppermute(down, axis, backward))  7.11 us
  transfers between devices with their start and end apart: 4, of which 3 were waited for; matrix products, arithmetic and copies ran while one was open for 1% of the time, Pallas kernels for 2%

profile of v3, /device:TPU:1, one launch (start us, length us, event | category | flops | bytes accessed | tf_op | source)
XLA Modules:
  0.0 117.8 jit_solution(17127252651840932876)
XLA Ops:
  0.6 0.0 copy-start.10
  0.6 1.1 slice_dynamic-update-slice_fusion
  1.7 0.0 copy-done.10
  1.7 0.1 copy.29
  1.9 0.0 copy-start.5
  1.9 0.1 fusion.4
  2.0 0.7 copy-done.5
  2.7 0.0 copy-start.6
  2.7 0.8 copy-done.6
  3.5 0.0 copy-start.7
  3.6 0.8 copy-done.7
  4.4 0.1 broadcast_select_fusion
  4.5 3.6 %collective-permute-start.1 = (f32[7,16,3,128]{3,2,1,0:T(4,128)S(1)}, f32[7,16,3,128]{3,2,1,0:T(4,128)S(1)}, u32[]{:S(2)}, u32[]{:S(2)}) collective-permute-start(f32[7,16,3,128]{3,2,1,0:T(4,128)S(1)} %broadcast_select_fusion), channel_id=1, source_target_pairs={{1,0},{2,1},{3,2},{0,3},{5,4},{6,5},{7,6},{4,7},{9,8},{10,9},{11,1... | collective-permute-start | bytes 516104 | tf_op jit(solution)/shard_map/ppermute | solution.py:307
  8.1 0.1 broadcast_select_fusion.1
  8.2 0.1 collective-permute-start
  8.3 0.8 constant_dynamic-update-slice_fusion.17
  9.1 0.1 pad.11.clone
  9.2 3.2 %collective-permute-done.1.yhigh = f32[7,16,3,128]{3,2,1,0:T(4,128)S(1)} collective-permute-done((f32[7,16,3,128]{3,2,1,0:T(4,128)S(1)}, f32[7,16,3,128]{3,2,1,0:T(4,128)S(1)}, u32[]{:S(2)}, u32[]{:S(2)}) %collective-permute-start.1) | collective-permute-done | bytes 172064 | tf_op jit(solution)/shard_map/ppermute | solution.py:307
  12.4 0.0 copy-start.8
  12.4 3.2 %collective-permute-done.ylow = f32[7,16,3,128]{3,2,1,0:T(4,128)S(1)} collective-permute-done((f32[7,16,3,128]{3,2,1,0:T(4,128)S(1)}, f32[7,16,3,128]{3,2,1,0:T(4,128)S(1)}, u32[]{:S(2)}, u32[]{:S(2)}) %collective-permute-start) | collective-permute-done | bytes 172064 | tf_op jit(solution)/shard_map/ppermute | solution.py:307
  15.6 0.0 copy-start.9
  15.7 0.0 copy-start.11
  15.7 0.0 copy-start.12
  15.7 0.1 maximum_select_fusion.1
  15.8 0.0 copy-done.8
  15.8 0.5 copy-done.9
  16.3 3.4 %collective-permute-start.2 = (f32[7,3,16,128]{3,2,1,0:T(8,128)S(1)}, f32[7,3,16,128]{3,2,1,0:T(8,128)S(1)}, u32[]{:S(2)}, u32[]{:S(2)}) collective-permute-start(f32[7,3,16,128]{3,2,1,0:T(8,128)S(1)} %get-tuple-element.42), channel_id=1, source_target_pairs={{0,4},{4,8},{8,12},{12,16},{16,20},{20,24},{24,28},{28,32},{32,36}... | collective-permute-start | bytes 516104 | tf_op jit(solution)/shard_map/ppermute | solution.py:307
  19.7 0.0 collective-permute-start.3
  19.7 0.0 copy-done.11
  19.7 0.0 copy-done.12
  19.7 0.0 copy-start.13
  19.7 0.6 pad.4.own_dir
  20.4 0.0 copy-done.13
  20.4 0.0 copy-start
  20.4 0.1 copy.32
  20.5 0.1 reshape.41.contact_ref
  20.6 0.0 copy-start.2
  20.6 0.5 copy-done
  21.1 0.2 copy-done.2
  21.3 1.9 %prep.1 = (s32[1,2048]{1,0:T(1,128)S(1)}, f32[3,8,128]{2,1,0:T(8,128)S(1)}, f32[8,128]{1,0:T(8,128)S(1)}) custom-call(s32[32]{0:T(128)S(1)} %reshape.41.contact_ref, s32[1,2048]{1,0:T(1,128)S(1)} %bitcast.53, f32[3,8,128]{2,1,0:T(8,128)S(1)} %get-tuple-element.44.pos_ref, f32[3,8,128]{2,1,0:T(8,128)S(1)} %get-tuple-element.43.vel_ref, f32[8,128]{1,0:T(8,128)S(1)} %bitcast.55), custom_call_target="tpu_custom_call" | custom-call | flops 1000000000 | bytes 1000000 | tf_op jit(solution)/shard_map/prep/pallas_call | solution.py:336
  23.2 0.0 copy-start.3
  23.2 0.6 copy-done.3
  23.8 0.0 collective-permute-done.2.xlow
  23.8 0.0 copy-start.14
  23.8 0.7 collective-permute-done.3.xhigh
  24.5 0.0 copy-start.15
  24.5 0.0 copy-done.14
  24.5 0.7 copy-done.15
  25.2 52.6 %fluid.1 = (f32[16,8,128]{2,1,0:T(8,128)}, f32[64,2,128]{2,1,0:T(2,128)}) custom-call(f32[3,16,8,128]{3,2,1,0:T(8,128)} %own_pos.1, f32[16,8,128]{2,1,0:T(8,128)} %own_press.1, f32[16,8,128]{2,1,0:T(8,128)} %own_src.1, f32[16,8,128]{2,1,0:T(8,128)} %own_res.1, f32[16,8,128]{2,1,0:T(8,128)} %pad.4.own_dir, f32[7,16,3,128]{3,2,1,0:T(4,128)} %copy-done.9, ...), custom_call_target="tpu_custom_call" | custom-call | flops 10000000000 | bytes 10000000 | tf_op jit(solution)/shard_map/fluid/pallas_call | solution.py:347
  77.8 22.1 %all_to_all.16 = f32[64,2,128]{2,1,0:T(2,128)S(1)} all-to-all(f32[64,2,128]{2,1,0:T(2,128)} %get-tuple-element.12), channel_id=1, replica_groups=mesh['blk'=64,'crs'=4] {'blk'}, dimensions={0} | all-to-all | bytes 131072 | tf_op jit(solution)/shard_map/all_to_all | solution.py:369
  99.9 0.1 reshape.47
  100.1 0.1 reshape.48.got_ref
  100.2 1.5 %grain.1 = (f32[3,1024]{1,0:T(4,128)}, f32[3,4096]{1,0:T(4,128)S(1)}) custom-call(f32[4,4096]{1,0:T(4,128)S(1)} %reshape.48.got_ref, f32[3,8,128]{2,1,0:T(8,128)S(1)} %get-tuple-element.13.base_ref, f32[8,128]{1,0:T(8,128)S(1)} %get-tuple-element.14.gain_ref), custom_call_target="tpu_custom_call" | custom-call | flops 1000000000 | bytes 1000000 | tf_op jit(solution)/shard_map/grain/pallas_call | solution.py:371
  101.7 0.1 reshape.49
  101.8 0.1 copy.34
  101.9 0.1 copy.35
  102.0 13.7 %all_to_all.17 = f32[64,1,192]{2,1,0:T(1,128)S(1)} all-to-all(f32[64,1,192]{2,1,0:T(1,128)S(1)} %copy.35), channel_id=1, replica_groups=mesh['blk'=64,'crs'=4] {'blk'}, dimensions={0} | all-to-all | bytes 98304 | tf_op jit(solution)/shard_map/all_to_all | solution.py:381
  115.6 0.0 copy-start.1
  115.6 0.0 copy-start.4
  115.7 0.7 copy-done.1
  116.3 0.0 copy-done.4
  116.4 1.5 %pick.1 = f32[3,2048]{1,0:T(4,128)} custom-call(f32[64,192]{1,0:T(8,128)S(1)} %bitcast.51, s32[1,2048]{1,0:T(1,128)S(1)} %bitcast.54, s32[1,2048]{1,0:T(1,128)S(1)} %copy-done.4), custom_call_target="tpu_custom_call" | custom-call | flops 1000000000 | bytes 1000000 | tf_op jit(solution)/shard_map/pick/pallas_call | solution.py:382
  (14 shorter events, 0.2 us)
Async XLA Ops:
  0.6 1.1 copy-start.10
  1.9 0.8 copy-start.5
  2.7 0.8 copy-start.6
  3.5 0.8 copy-start.7
  4.5 7.9 %collective-permute-start.1 = (f32[7,16,3,128]{3,2,1,0:T(4,128)S(1)}, f32[7,16,3,128]{3,2,1,0:T(4,128)S(1)}, u32[]{:S(2)}, u32[]{:S(2)}) collective-permute-start(f32[7,16,3,128]{3,2,1,0:T(4,128)S(1)} %broadcast_select_fusion), channel_id=1, source_target_pairs={{1,0},{2,1},{3,2},{0,3},{5,4},{6,5},{7,6},{4,7},{9,8},{10,9},{11,1... | collective-permute-start | bytes 516104 | tf_op jit(solution)/shard_map/ppermute | solution.py:307
  8.2 7.4 %collective-permute-start = (f32[7,16,3,128]{3,2,1,0:T(4,128)S(1)}, f32[7,16,3,128]{3,2,1,0:T(4,128)S(1)}, u32[]{:S(2)}, u32[]{:S(2)}) collective-permute-start(f32[7,16,3,128]{3,2,1,0:T(4,128)S(1)} %broadcast_select_fusion.1), channel_id=1, source_target_pairs={{0,1},{1,2},{2,3},{3,0},{4,5},{5,6},{6,7},{7,4},{8,9},{9,10},{10,1... | collective-permute-start | bytes 516104 | tf_op jit(solution)/shard_map/ppermute | solution.py:307
  12.4 3.4 %copy-start.8 = (f32[7,16,3,128]{3,2,1,0:T(4,128)}, f32[7,16,3,128]{3,2,1,0:T(4,128)S(1)}, u32[]{:S(2)}) copy-start(f32[7,16,3,128]{3,2,1,0:T(4,128)S(1)} %collective-permute-done.1.yhigh) | copy-start | bytes 516100
  15.6 0.7 copy-start.9
  15.7 4.1 %copy-start.11 = (f32[3,1024]{1,0:T(4,128)S(1)}, f32[3,1024]{1,0:T(4,128)}, u32[]{:S(2)}) copy-start(f32[3,1024]{1,0:T(4,128)} %param.23) | copy-start | bytes 36868
  15.7 4.0 %copy-start.12 = (f32[3,1024]{1,0:T(4,128)S(1)}, f32[3,1024]{1,0:T(4,128)}, u32[]{:S(2)}) copy-start(f32[3,1024]{1,0:T(4,128)} %param.22) | copy-start | bytes 36868
  16.3 7.5 %collective-permute-start.2 = (f32[7,3,16,128]{3,2,1,0:T(8,128)S(1)}, f32[7,3,16,128]{3,2,1,0:T(8,128)S(1)}, u32[]{:S(2)}, u32[]{:S(2)}) collective-permute-start(f32[7,3,16,128]{3,2,1,0:T(8,128)S(1)} %get-tuple-element.42), channel_id=1, source_target_pairs={{0,4},{4,8},{8,12},{12,16},{16,20},{20,24},{24,28},{28,32},{32,36}... | collective-permute-start | bytes 516104 | tf_op jit(solution)/shard_map/ppermute | solution.py:307
  19.7 4.8 %collective-permute-start.3 = (f32[7,3,16,128]{3,2,1,0:T(8,128)S(1)}, f32[7,3,16,128]{3,2,1,0:T(8,128)S(1)}, u32[]{:S(2)}, u32[]{:S(2)}) collective-permute-start(f32[7,3,16,128]{3,2,1,0:T(8,128)S(1)} %get-tuple-element.41), channel_id=1, source_target_pairs={{4,0},{8,4},{12,8},{16,12},{20,16},{24,20},{28,24},{32,28},{36,32}... | collective-permute-start | bytes 516104 | tf_op jit(solution)/shard_map/ppermute | solution.py:307
  19.7 0.7 copy-start.13
  20.4 0.7 copy-start
  20.6 0.7 copy-start.2
  23.2 0.6 copy-start.3
  23.8 0.7 copy-start.14
  24.5 0.7 copy-start.15
  115.6 0.7 copy-start.1
  115.6 0.7 copy-start.4

commit v4 on v3

--- a/solution.py
+++ b/solution.py
@@ -47,6 +47,48 @@
     return left, right
 
 
+OWN = slice(HALO, HALO + TX)
+
+
+def pack_kernel(pos_hbm, press_hbm, src_hbm, res_hbm, near_ref, up_ref, down_ref, way_ref, pos, rest, named_v, sems):
+    gets = [
+        pltpu.make_async_copy(pos_hbm, pos, sems.at[0]),
+        pltpu.make_async_copy(press_hbm, rest.at[0], sems.at[1]),
+        pltpu.make_async_copy(src_hbm, rest.at[1], sems.at[2]),
+        pltpu.make_async_copy(res_hbm, rest.at[2], sems.at[3]),
+    ]
+    for get in gets:
+        get.start()
+    named_v[...] = jnp.zeros_like(named_v)
+    named_v[:, :, :TX] = near_ref[...]
+    ways = []
+    for k in range(KN):
+        named = named_v[k]
+        ext_x = lax.shift_right_logical(named * 205, 11)
+        ways.append((ext_x - iota((TY, L), 1)) * 3 + named - (TY + 2) * ext_x - iota((TY, L), 0))
+    lane = iota((TY, L), 1)
+    for x in range(TX):
+        row = jnp.zeros((TY, L), I32)
+        for k in range(KN):
+            row = jnp.where(lane == k, pltpu.roll(ways[k], (k - x) % L, 1), row)
+        way_ref[x] = row.astype(F32)
+    top = lax.axis_index("crs") == lax.axis_size("crs") - 1
+    bottom = lax.axis_index("crs") == 0
+    for get in gets:
+        get.wait()
+    for p in range(PLANES):
+        plane = pos.at[p] if p < 3 else way_ref if p == 6 else rest.at[p - 3]
+        up_ref[p] = jnp.where(top, 0.0, plane[:, TY - HALO :, :])
+        down_ref[p] = jnp.where(bottom, 0.0, plane[:, :HALO, :])
+
+
+def build_half(xyz, stage):
+    left, right = distance_rows(xyz)
+    for k, row in enumerate(left + right):
+        stage[pl.ds(k if k < len(left) else k - len(left) + K, 8, stride=2 * K), :] = row
+    return stage[...].astype(BF16).reshape(8, 2 * K, L)
+
+
 def store_rows(stage, rows, first, count):
     for k, row in enumerate(rows):
         stage[pl.ds(first * K + k, count, stride=K), :] = row
@@ -61,7 +103,50 @@
     return jnp.sum(acc.T, axis=0, keepdims=True)
 
 
-def prep_kernel(contact_ref, owner_ref, pos_ref, vel_ref, mass_ref, rank_ref, base_ref, gain_ref, stage_a, stage_b):
+def side_kernel(yhigh, ylow, out_ref, ext, stage, lr, sems):
+    stage[...] = jnp.zeros_like(stage)
+    ext[...] = jnp.zeros_like(ext)
+    for c in range(3):
+        for x in range(TX):
+            ext[c, x, :HALO, :] = yhigh[c, x]
+            ext[c, x, 8 - HALO :, :] = ylow[c, x]
+    quarter = TX // 4
+
+    def send(i):
+        rows = pl.ds(i * quarter, quarter)
+        return pltpu.make_async_copy(lr.at[rows], out_ref.at[rows], sems.at[i])
+
+    def build(i, _):
+        for e in range(quarter):
+            x = i * quarter + e
+            lr[x] = build_half([ext[c, x] for c in range(3)], stage)
+        send(i).start()
+        return 0
+
+    lax.fori_loop(0, 4, build, 0)
+    for i in range(4):
+        send(i).wait()
+
+
+def prep_kernel(
+    contact_ref, owner_ref, pos_ref, vel_ref, mass_ref, own_pos, own_press, own_src, own_res, own_way,
+    rank_ref, base_ref, gain_ref, lr_ref, last_ref, first_ref,
+    stage_a, stage_b, vel, stage, lr, sem,
+):
+    for p, plane in enumerate((own_pos.at[0], own_pos.at[1], own_pos.at[2], own_press, own_src, own_res, own_way)):
+        last_ref[p] = plane[TX - HALO :]
+        first_ref[p] = plane[:HALO]
+    stage[...] = jnp.zeros_like(stage)
+
+    def build(i, _):
+        for e in range(4):
+            x = i * 4 + e
+            lr[x] = build_half([own_pos[c, x] for c in range(3)], stage)
+        return 0
+
+    lax.fori_loop(0, TX // 4, build, 0)
+    send = pltpu.make_async_copy(lr, lr_ref, sem)
+    send.start()
     owner = owner_ref[...]
     upper = (iota((256, 256), 0) < iota((256, 256), 1)).astype(BF16)
     every = jnp.ones((256, 256), BF16)
@@ -72,10 +157,15 @@
         before = dot(hot, upper, NN) + carry
         rank_ref[:, q : q + 256] = jnp.sum(jnp.where(named, before, 0.0), axis=0, keepdims=True).astype(I32)
         carry = carry + dot(hot, every, NN)
-    tiles = vel_ref.shape[1]
+    tiles = mass_ref.shape[0]
     stage_a[...] = jnp.zeros_like(stage_a)
     stage_b[...] = jnp.zeros_like(stage_b)
-    left, right = distance_rows([pos_ref[c] for c in range(3)])
+    def tiled(ref, c):
+        return jnp.concatenate([ref[c : c + 1, t * L : (t + 1) * L] for t in range(tiles)], axis=0)
+
+    for c in range(3):
+        vel[c] = tiled(vel_ref, c)
+    left, right = distance_rows([tiled(pos_ref, c) for c in range(3)])
     store_rows(stage_a, left, 0, tiles)
     store_rows(stage_b, right, 0, tiles)
     gain = 0.1 / mass_ref[...]
@@ -85,34 +175,42 @@
         total = jnp.zeros((L, L), F32)
         applied = [jnp.zeros((L, L), F32) for _ in range(3)]
         for k in range(4):
-            n = contact_ref[t * 4 + k]
+            n = contact_ref[k, t]
             b = stage_b[pl.ds(pl.multiple_of(n * K, K), K), :].astype(BF16)
             w = cube(dot(a, b, TN))
             total = total + w
             for c in range(3):
-                applied[c] = applied[c] + w * vel_ref[c, pl.ds(n, 1), :]
+                applied[c] = applied[c] + w * vel[c, pl.ds(n, 1), :]
         total = column_sum(total)
         for c in range(3):
-            own = vel_ref[c, t : t + 1, :]
+            own = vel[c, t : t + 1, :]
             contact = (column_sum(applied[c]) - total * own) * (4.0 / 512)
             base_ref[c, t : t + 1, :] = own + gain[t : t + 1, :] * contact
+    send.wait()
 
 
 def fluid_kernel(
-    own_pos, own_press, own_src, own_res, own_dir, ylow, yhigh, xlow, xhigh, owner_ref, rank_ref, fluid_ref, grain_ref, normal_ref,
+    own_press, own_src, own_res, own_way, ylow, yhigh, xlow, xhigh, lr_own, lr_side, owner_ref, rank_ref, fluid_ref, grain_ref, normal_ref,
     press_ref, send_ref,
-    ext, near_v, near_s, stage, left_s, right_s, num_s, deg_s, kept, sem,
+    ext, near_v, near_s, stage, lr, num_s, deg_s, kept, sem, in_sem,
 ):
     blk, crs = lax.axis_index("blk"), lax.axis_index("crs")
     blks, crss = lax.axis_size("blk"), lax.axis_size("crs")
-    ext[:, HALO * EY : (HALO + TX) * EY, :] = jnp.zeros((PLANES, TX * EY, L), F32)
+    gets = [
+        pltpu.make_async_copy(lr_own, lr.at[OWN, :TY], in_sem.at[0]),
+        pltpu.make_async_copy(lr_side, lr.at[OWN, TY:], in_sem.at[1]),
+    ]
+    for get in gets:
+        get.start()
+    own = (own_press, own_src, own_res, own_way)
+    ext[3:, HALO * EY : (HALO + TX) * EY, :] = jnp.zeros((len(own), TX * EY, L), F32)
     for x in range(HALO):
         for p in range(PLANES):
             ext[p, x * EY : (x + 1) * EY, :] = xlow[p, x]
             ext[p, (HALO + TX + x) * EY : (HALO + TX + x + 1) * EY, :] = xhigh[p, x]
     for x in range(TX):
         r = (HALO + x) * EY
-        for p, plane in enumerate((own_pos.at[0], own_pos.at[1], own_pos.at[2], own_press, own_src, own_res, own_dir)):
+        for p, plane in enumerate(own, 3):
             ext[p, r : r + TY, :] = plane[x]
             ext[p, r + TY : r + TY + HALO, :] = yhigh[p, x]
             ext[p, r + EY - HALO : r + EY, :] = ylow[p, x]
@@ -130,25 +228,25 @@
     copy = pltpu.make_async_copy(near_v, near_s, sem)
     copy.start()
 
-    def build(ex, _):
-        r = pl.multiple_of(ex * EY, EY)
-        left, right = distance_rows([ext[c, pl.ds(r, EY), :] for c in range(3)])
-        for rows, target in ((left, left_s), (right, right_s)):
-            for half in range(0, EY, 8):
-                store_rows(stage, [row[half : half + 8] for row in rows], half, 8)
-            target[pl.ds(pl.multiple_of(r * K, EY * K), EY * K), :] = stage[...].astype(BF16)
+    def build(i, _):
+        ex = i + jnp.where(i >= HALO, TX, 0)
+        for half in (0, 8):
+            r = pl.multiple_of(ex * EY + half, 8)
+            lr[ex, half : half + 8] = build_half([ext[c, pl.ds(r, 8), :] for c in range(3)], stage)
         return 0
 
-    lax.fori_loop(0, EX, build, 0)
+    lax.fori_loop(0, 2 * HALO, build, 0)
+    for get in gets:
+        get.wait()
     copy.wait()
 
     def one_tile(t, with_deg, slot=None):
-        a = left_s[pl.ds(pl.multiple_of(t * K, K), K), :]
+        a = lr[lax.shift_right_logical(t, 4), t & (EY - 1), :K, :]
         acc = jnp.zeros((L, L), F32)
         tot = jnp.zeros((L, L), F32)
         for k in range(0, KN, 2):
             n = [near_s[t, k + e] for e in range(2)]
-            b = jnp.concatenate([right_s[pl.ds(pl.multiple_of(m * K, K), K), :] for m in n], axis=1)
+            b = jnp.concatenate([lr[lax.shift_right_logical(m, 4), m & (EY - 1), K:, :] for m in n], axis=1)
             w = cube(dot(a, b, TN))
             for e in range(2):
                 part = w[:, e * L : (e + 1) * L]
@@ -283,6 +381,7 @@
 
 VMEM = pl.BlockSpec(memory_space=pltpu.VMEM)
 SMEM = pl.BlockSpec(memory_space=pltpu.SMEM)
+HBM = pl.BlockSpec(memory_space=pltpu.HBM)
 
 
 def shape(*dims, dtype=F32):
@@ -297,14 +396,6 @@
     count = lax.axis_size(axis)
     forward = [(i, (i + 1) % count) for i in range(count)]
     return forward, [(b, a) for a, b in forward]
-
-
-def exchange(axis, up, down):
-    forward, backward = shifts(axis)
-    here = lax.axis_index(axis)
-    up = jnp.where(here == lax.axis_size(axis) - 1, 0.0, up)
-    down = jnp.where(here == 0, 0.0, down)
-    return lax.ppermute(up, axis, forward), lax.ppermute(down, axis, backward)
 
 
 def on_device(positions, pressure_start, source, resist, neighbour_tiles, pair_owner, pair_fluid, pair_grain, pair_normal,
@@ -313,58 +404,77 @@
     owner = pair_owner.reshape(1, pairs)
     fluid = pair_fluid.reshape(1, pairs)
     grain = pair_grain.reshape(1, pairs)
-    here_x = jnp.arange(TX, dtype=I32)[:, None, None]
-    here_y = jnp.arange(TY, dtype=I32)[None, :, None]
-    way = (neighbour_tiles // (TY + 2) - here_x) * 3 + neighbour_tiles % (TY + 2) - here_y
-    way = jnp.pad(way.astype(F32), ((0, 0), (0, 0), (0, L - KN)))
-
-    def planes(xs, ys):
-        return jnp.concatenate(
-            [positions[:, xs, ys], pressure_start[None, xs, ys], source[None, xs, ys], resist[None, xs, ys], way[None, xs, ys]], axis=0
-        )
-
-    every, first, last = slice(None), slice(0, HALO), slice(-HALO, None)
-    ylow, yhigh = exchange("crs", planes(every, last), planes(every, first))
-    gap = jnp.zeros((PLANES, HALO, EY - TY - 2 * HALO, L), F32)
-
-    def wide(xs):
-        return jnp.concatenate([planes(xs, every), yhigh[:, xs], gap, ylow[:, xs]], axis=2)
-
-    xlow, xhigh = exchange("blk", wide(last), wide(first))
-
+    semaphore = pltpu.SemaphoreType.DMA
+    params = pltpu.CompilerParams(vmem_limit_bytes=62 << 20)
+    rim_y, rim_x = shape(PLANES, TX, HALO, L), shape(PLANES, HALO, TY, L)
+    up, down, way = pl.pallas_call(
+        pack_kernel,
+        out_shape=(rim_y, rim_y, shape(TX, TY, L)),
+        in_specs=[HBM] * 4 + [VMEM],
+        out_specs=(VMEM,) * 3,
+        scratch_shapes=[pltpu.VMEM((3, TX, TY, L), F32), pltpu.VMEM((3, TX, TY, L), F32), pltpu.VMEM((KN, TY, L), I32), semaphore((4,))],
+        compiler_params=params,
+        cost_estimate=cost(10**6, 10**6),
+        name="pack",
+    )(positions, pressure_start, source, resist, neighbour_tiles.transpose(2, 1, 0))
+    forward, backward = shifts("crs")
+    ylow = lax.ppermute(up, "crs", forward)
+    yhigh = lax.ppermute(down, "crs", backward)
     grain_tiles = grain_mass.shape[0] // L
-    rank, base, gain = pl.pallas_call(
+    half = shape(TX, 8, 2 * K, L, dtype=BF16)
+    half_scratch = [pltpu.VMEM((8 * 2 * K, L), F32), pltpu.VMEM((TX, 8, 2 * K, L), BF16)]
+    rank, base, gain, lr_own, last, first = pl.pallas_call(
         prep_kernel,
-        out_shape=(shape(1, pairs, dtype=I32), shape(3, grain_tiles, L), shape(grain_tiles, L)),
-        in_specs=[SMEM] + [VMEM] * 4,
-        out_specs=(VMEM,) * 3,
-        scratch_shapes=[pltpu.VMEM((grain_tiles * K, L), F32)] * 2,
-        compiler_params=pltpu.CompilerParams(vmem_limit_bytes=32 << 20),
+        out_shape=(shape(1, pairs, dtype=I32), shape(3, grain_tiles, L), shape(grain_tiles, L), half, rim_x, rim_x),
+        in_specs=[SMEM] + [VMEM] * 9,
+        out_specs=(VMEM, VMEM, VMEM, HBM, VMEM, VMEM),
+        scratch_shapes=[pltpu.VMEM((grain_tiles * K, L), F32)] * 2 + [pltpu.VMEM((3, grain_tiles, L), F32)] + half_scratch + [semaphore],
+        compiler_params=params,
         cost_estimate=cost(10**9, 10**6),
         name="prep",
-    )(contact_tiles.reshape(-1), owner, grain_positions.reshape(3, grain_tiles, L), grain_velocity.reshape(3, grain_tiles, L), grain_mass.reshape(grain_tiles, L))
+    )(contact_tiles.T, owner, grain_positions, grain_velocity, grain_mass.reshape(grain_tiles, L), positions, pressure_start, source, resist, way)
+    gap = jnp.zeros((PLANES, HALO, EY - TY - 2 * HALO, L), F32)
+
+    def wide(middle, xs):
+        return jnp.concatenate([middle, yhigh[:, xs], gap, ylow[:, xs]], axis=2)
+
+    forward, backward = shifts("blk")
+    here, count = lax.axis_index("blk"), lax.axis_size("blk")
+    xlow = lax.ppermute(jnp.where(here == count - 1, 0.0, wide(last, slice(-HALO, None))), "blk", forward)
+    xhigh = lax.ppermute(jnp.where(here == 0, 0.0, wide(first, slice(0, HALO))), "blk", backward)
+
+    lr_side = pl.pallas_call(
+        side_kernel,
+        out_shape=half,
+        in_specs=[VMEM] * 2,
+        out_specs=HBM,
+        scratch_shapes=[pltpu.VMEM((3, TX, 8, L), F32), *half_scratch, semaphore((4,))],
+        compiler_params=params,
+        cost_estimate=cost(10**9, 10**6),
+        name="side",
+    )(yhigh, ylow)
 
     press, send = pl.pallas_call(
         fluid_kernel,
         out_shape=(shape(TX, TY, L), shape(64, 2, L)),
-        in_specs=[VMEM] * 14,
+        in_specs=[VMEM] * 8 + [HBM] * 2 + [VMEM] * 5,
         out_specs=(VMEM,) * 2,
         scratch_shapes=[
             pltpu.VMEM((PLANES, TILES, L), F32),
             pltpu.VMEM((TILES, L), I32),
             pltpu.SMEM((TILES, L), I32),
-            pltpu.VMEM((EY * K, L), F32),
-            pltpu.VMEM((TILES * K, L), BF16),
-            pltpu.VMEM((TILES * K, L), BF16),
+            pltpu.VMEM((8 * 2 * K, L), F32),
+            pltpu.VMEM((EX, EY, 2 * K, L), BF16),
             pltpu.VMEM((TILES, L), F32),
             pltpu.VMEM((TILES, L), F32),
             pltpu.VMEM((TX * TY, KN, L, L), F32),
-            pltpu.SemaphoreType.DMA,
+            semaphore,
+            semaphore((2,)),
         ],
-        compiler_params=pltpu.CompilerParams(vmem_limit_bytes=60 << 20),
+        compiler_params=pltpu.CompilerParams(vmem_limit_bytes=62 << 20),
         cost_estimate=cost(10**10, 10**7),
         name="fluid",
-    )(positions, pressure_start, source, resist, way, ylow, yhigh, xlow, xhigh, owner, rank, fluid, grain, pair_normal)
+    )(pressure_start, source, resist, way, ylow, yhigh, xlow, xhigh, lr_own, lr_side, owner, rank, fluid, grain, pair_normal)
 
     got = lax.all_to_all(send, "blk", 0, 0, tiled=True)
     got = got.reshape(64, 4, CAP).swapaxes(0, 1).reshape(4, 64 * CAP)

time: 118 us -> 115 us (0.975)
  Pallas kernels: 57.5 us -> 65.8 us
  local copies, waits for them, and re-layouts: 9.2 us -> 1.4 us
  waiting for transfers between devices: 7.11 us -> 2.38 us
    unnamed x43 -> x17, local copies, waits for them, and re-layouts: 7.78 us -> 0.72 us
    pallas_call x0 -> x2, Pallas kernels: none -> 6.57 us  [the longest x1 3.85 us: on_device(): pl.pallas_call(side_kernel, out_shape=half, in_specs=[VMEM] * 2, out_spec...]
    ppermute x4, waiting for transfers between devices: 7.11 us -> 2.38 us  [the longest x1 1.43 us: on_device(): ylow = lax.ppermute(up, 'crs', forward)]
    pallas_call x1, Pallas kernels: 1.94 us -> 6.01 us  [on_device(): pl.pallas_call(prep_kernel, out_shape=(shape(1, pairs, dtype=I32), shape(...]
    pallas_call x1, Pallas kernels: 52.6 us -> 50.3 us  [on_device(): pl.pallas_call(fluid_kernel, out_shape=(shape(TX, TY, L), shape(64, 2, L)...]
  transfers between devices with their start and end apart: 4 -> 4, of which waited for: 3 -> 2; matrix products, arithmetic and copies ran while one was open for 1% -> 0% of each run, Pallas kernels for 2% -> 9%
where the time goes in v4:
time: 115 us; the launch traced here: 114 us
  Pallas kernels  65.8 us (57%)
  blocking collectives  35.5 us (31%)
  starting transfers between devices  7.11 us (6%)
  waiting for transfers between devices  2.38 us (2%)
  local copies, waits for them, and re-layouts  1.4 us (1%)
    pallas_call x1, Pallas kernels, on_device(): pl.pallas_call(fluid_kernel, out_shape=(shape(TX, TY, L), shape(64, 2, L)...  50.3 us
    all_to_all x1, blocking collectives, on_device(): got = lax.all_to_all(send, 'blk', 0, 0, tiled=True)  21.9 us
    all_to_all x1, blocking collectives, on_device(): seen = lax.all_to_all(back, 'blk', 0, 0, tiled=True)  13.7 us
    pallas_call x1, Pallas kernels, on_device(): pl.pallas_call(prep_kernel, out_shape=(shape(1, pairs, dtype=I32), shape(...  6.01 us
    pallas_call x1, Pallas kernels, on_device(): pl.pallas_call(side_kernel, out_shape=half, in_specs=[VMEM] * 2, out_spec...  3.85 us
    ppermute x1, starting transfers between devices, on_device(): yhigh = lax.ppermute(down, 'crs', backward)  3.64 us
    ppermute x1, starting transfers between devices, on_device(): lax.ppermute(jnp.where(here == count - 1, 0.0, wide(last, slice(-HALO, No...  3.46 us
    pallas_call x1, Pallas kernels, on_device(): pl.pallas_call(pack_kernel, out_shape=(rim_y, rim_y, shape(TX, TY, L)), i...  2.72 us
  transfers between devices with their start and end apart: 4, of which 2 were waited for; matrix products, arithmetic and copies ran while one was open for 0% of the time, Pallas kernels for 9%

profile of v4, /device:TPU:1, one launch (start us, length us, event | category | flops | bytes accessed | tf_op | source)
XLA Modules:
  0.0 114.2 jit_solution(2499276795672514854)
XLA Ops:
  0.6 2.7 %pack.1 = (f32[7,16,3,128]{3,2,1,0:T(4,128)}, f32[7,16,3,128]{3,2,1,0:T(4,128)}, f32[16,8,128]{2,1,0:T(8,128)}) custom-call(f32[3,16,8,128]{3,2,1,0:T(8,128)} %own_pos.1, f32[16,8,128]{2,1,0:T(8,128)} %own_press.3, f32[16,8,128]{2,1,0:T(8,128)} %own_src.3, f32[16,8,128]{2,1,0:T(8,128)} %own_res.3, s32[6,8,16]{2,1,0:T(8,128)} %bitcast.21), custom_call_target="tpu_custom_call" | custom-call | flops 1000000 | bytes 1000000 | tf_op jit(solution)/shard_map/pack/pallas_call | solution.py:410
  3.4 3.6 %collective-permute-start.1 = (f32[7,16,3,128]{3,2,1,0:T(4,128)}, f32[7,16,3,128]{3,2,1,0:T(4,128)S(1)}, u32[]{:S(2)}, u32[]{:S(2)}) collective-permute-start(f32[7,16,3,128]{3,2,1,0:T(4,128)} %get-tuple-element.18), channel_id=1, source_target_pairs={{1,0},{2,1},{3,2},{0,3},{5,4},{6,5},{7,6},{4,7},{9,8},{10,9},{11,1... | collective-permute-start | bytes 516104 | tf_op jit(solution)/shard_map/ppermute | solution.py:422
  7.0 0.0 collective-permute-start
  7.0 0.1 pad.6.clone
  7.1 6.0 %prep.1 = (s32[1,2048]{1,0:T(1,128)}, f32[3,8,128]{2,1,0:T(8,128)}, f32[8,128]{1,0:T(8,128)}, bf16[16,8,64,128]{3,2,1,0:T(8,128)(2,1)}, f32[7,3,8,128]{3,2,1,0:T(8,128)}, /*index=5*/f32[7,3,8,128]{3,2,1,0:T(8,128)}) custom-call(s32[4,8]{1,0:T(4,128)} %bitcast.25, s32[1,2048]{1,0:T(1,128)} %bitcast.16, f32[3,1024]{1,0:T(4,128)} %pos_ref.1, ...), custom_call_target="tpu_custom_call" | custom-call | flops 1000000000 | bytes 1000000 | tf_op jit(solution)/shard_map/prep/pallas_call | solution.py:426
  13.1 0.0 collective-permute-done.1.yhigh
  13.1 0.0 copy-start.4
  13.1 1.4 %collective-permute-done.ylow = f32[7,16,3,128]{3,2,1,0:T(4,128)S(1)} collective-permute-done((f32[7,16,3,128]{3,2,1,0:T(4,128)}, f32[7,16,3,128]{3,2,1,0:T(4,128)S(1)}, u32[]{:S(2)}, u32[]{:S(2)}) %collective-permute-start) | collective-permute-done | bytes 172064 | tf_op jit(solution)/shard_map/ppermute | solution.py:421
  14.6 0.0 copy-start.5
  14.6 1.1 maximum_select_fusion.1
  15.7 3.5 %collective-permute-start.2 = (f32[7,3,16,128]{3,2,1,0:T(8,128)S(1)}, f32[7,3,16,128]{3,2,1,0:T(8,128)S(1)}, u32[]{:S(2)}, u32[]{:S(2)}) collective-permute-start(f32[7,3,16,128]{3,2,1,0:T(8,128)S(1)} %get-tuple-element.34), channel_id=1, source_target_pairs={{0,4},{4,8},{8,12},{12,16},{16,20},{20,24},{24,28},{28,32},{32,36}... | collective-permute-start | bytes 516104 | tf_op jit(solution)/shard_map/ppermute | solution.py:443
  19.2 0.0 collective-permute-start.3
  19.2 0.0 copy-done.4
  19.2 0.0 copy-done.5
  19.2 3.9 %side.1.lr_side = bf16[16,8,64,128]{3,2,1,0:T(8,128)(2,1)} custom-call(f32[7,16,3,128]{3,2,1,0:T(4,128)} %copy-done.4, f32[7,16,3,128]{3,2,1,0:T(4,128)} %copy-done.5), custom_call_target="tpu_custom_call" | custom-call | flops 1000000000 | bytes 1000000 | tf_op jit(solution)/shard_map/side/pallas_call | solution.py:446
  23.1 0.0 collective-permute-done.2.xlow
  23.1 0.0 copy-start.6
  23.1 0.9 collective-permute-done.3.xhigh
  24.0 0.0 copy-start.7
  24.0 0.0 copy-done.6
  24.0 0.7 copy-done.7
  24.7 0.0 copy-start.1
  24.7 0.0 copy-start.3
  24.7 50.3 %fluid.1 = (f32[16,8,128]{2,1,0:T(8,128)}, f32[64,2,128]{2,1,0:T(2,128)}) custom-call(f32[16,8,128]{2,1,0:T(8,128)} %own_press.3, f32[16,8,128]{2,1,0:T(8,128)} %own_src.3, f32[16,8,128]{2,1,0:T(8,128)} %own_res.3, f32[16,8,128]{2,1,0:T(8,128)} %get-tuple-element.16.own_way, f32[7,16,3,128]{3,2,1,0:T(4,128)} %copy-done.5, f32[7,16,3,128]{3,2,1,0:T(4,128)} %copy-done.4, ...), custom_call_target="tpu_custom_call" | custom-call | flops 10000000000 | bytes 10000000 | tf_op jit(solution)/shard_map/fluid/pallas_call | solution.py:457
  75.0 21.9 %all_to_all.16 = f32[64,2,128]{2,1,0:T(2,128)S(1)} all-to-all(f32[64,2,128]{2,1,0:T(2,128)} %get-tuple-element.24), channel_id=1, replica_groups=mesh['blk'=64,'crs'=4] {'blk'}, dimensions={0} | all-to-all | bytes 131072 | tf_op jit(solution)/shard_map/all_to_all | solution.py:479
  96.9 0.1 reshape.35
  97.1 0.1 reshape.36.got_ref
  97.2 0.0 copy-done.1
  97.2 0.0 copy-done.3
  97.2 0.0 copy-start
  97.2 0.0 copy-start.2
  97.2 1.5 %grain.1 = (f32[3,1024]{1,0:T(4,128)}, f32[3,4096]{1,0:T(4,128)S(1)}) custom-call(f32[4,4096]{1,0:T(4,128)S(1)} %reshape.36.got_ref, f32[3,8,128]{2,1,0:T(8,128)S(1)} %copy-done.1, f32[8,128]{1,0:T(8,128)S(1)} %copy-done.3), custom_call_target="tpu_custom_call" | custom-call | flops 1000000000 | bytes 1000000 | tf_op jit(solution)/shard_map/grain/pallas_call | solution.py:481
  98.7 0.1 reshape.37
  98.8 0.1 copy.22
  98.9 0.1 copy.23
  99.0 13.7 %all_to_all.17 = f32[64,1,192]{2,1,0:T(1,128)S(1)} all-to-all(f32[64,1,192]{2,1,0:T(1,128)S(1)} %copy.23), channel_id=1, replica_groups=mesh['blk'=64,'crs'=4] {'blk'}, dimensions={0} | all-to-all | bytes 98304 | tf_op jit(solution)/shard_map/all_to_all | solution.py:491
  112.7 0.0 copy-done
  112.7 0.0 copy-done.2
  112.7 1.5 %pick.1 = f32[3,2048]{1,0:T(4,128)} custom-call(f32[64,192]{1,0:T(8,128)S(1)} %bitcast.15, s32[1,2048]{1,0:T(1,128)S(1)} %bitcast.18, s32[1,2048]{1,0:T(1,128)S(1)} %copy-done.2), custom_call_target="tpu_custom_call" | custom-call | flops 1000000000 | bytes 1000000 | tf_op jit(solution)/shard_map/pick/pallas_call | solution.py:492
  (5 shorter events, 0.0 us)
Async XLA Ops:
  3.4 9.7 %collective-permute-start.1 = (f32[7,16,3,128]{3,2,1,0:T(4,128)}, f32[7,16,3,128]{3,2,1,0:T(4,128)S(1)}, u32[]{:S(2)}, u32[]{:S(2)}) collective-permute-start(f32[7,16,3,128]{3,2,1,0:T(4,128)} %get-tuple-element.18), channel_id=1, source_target_pairs={{1,0},{2,1},{3,2},{0,3},{5,4},{6,5},{7,6},{4,7},{9,8},{10,9},{11,1... | collective-permute-start | bytes 516104 | tf_op jit(solution)/shard_map/ppermute | solution.py:422
  7.0 7.6 %collective-permute-start = (f32[7,16,3,128]{3,2,1,0:T(4,128)}, f32[7,16,3,128]{3,2,1,0:T(4,128)S(1)}, u32[]{:S(2)}, u32[]{:S(2)}) collective-permute-start(f32[7,16,3,128]{3,2,1,0:T(4,128)} %get-tuple-element.17), channel_id=1, source_target_pairs={{0,1},{1,2},{2,3},{3,0},{4,5},{5,6},{6,7},{7,4},{8,9},{9,10},{10,1... | collective-permute-start | bytes 516104 | tf_op jit(solution)/shard_map/ppermute | solution.py:421
  13.1 6.1 %copy-start.4 = (f32[7,16,3,128]{3,2,1,0:T(4,128)}, f32[7,16,3,128]{3,2,1,0:T(4,128)S(1)}, u32[]{:S(2)}) copy-start(f32[7,16,3,128]{3,2,1,0:T(4,128)S(1)} %collective-permute-done.1.yhigh) | copy-start | bytes 516100
  14.6 4.6 %copy-start.5 = (f32[7,16,3,128]{3,2,1,0:T(4,128)}, f32[7,16,3,128]{3,2,1,0:T(4,128)S(1)}, u32[]{:S(2)}) copy-start(f32[7,16,3,128]{3,2,1,0:T(4,128)S(1)} %collective-permute-done.ylow) | copy-start | bytes 516100
  15.7 7.3 %collective-permute-start.2 = (f32[7,3,16,128]{3,2,1,0:T(8,128)S(1)}, f32[7,3,16,128]{3,2,1,0:T(8,128)S(1)}, u32[]{:S(2)}, u32[]{:S(2)}) collective-permute-start(f32[7,3,16,128]{3,2,1,0:T(8,128)S(1)} %get-tuple-element.34), channel_id=1, source_target_pairs={{0,4},{4,8},{8,12},{12,16},{16,20},{20,24},{24,28},{28,32},{32,36}... | collective-permute-start | bytes 516104 | tf_op jit(solution)/shard_map/ppermute | solution.py:443
  19.2 4.8 %collective-permute-start.3 = (f32[7,3,16,128]{3,2,1,0:T(8,128)S(1)}, f32[7,3,16,128]{3,2,1,0:T(8,128)S(1)}, u32[]{:S(2)}, u32[]{:S(2)}) collective-permute-start(f32[7,3,16,128]{3,2,1,0:T(8,128)S(1)} %get-tuple-element.33), channel_id=1, source_target_pairs={{4,0},{8,4},{12,8},{16,12},{20,16},{24,20},{28,24},{32,28},{36,32}... | collective-permute-start | bytes 516104 | tf_op jit(solution)/shard_map/ppermute | solution.py:444
  23.1 1.0 copy-start.6
  24.0 0.7 copy-start.7
  24.7 72.5 %copy-start.1 = (f32[3,8,128]{2,1,0:T(8,128)S(1)}, f32[3,8,128]{2,1,0:T(8,128)}, u32[]{:S(2)}) copy-start(f32[3,8,128]{2,1,0:T(8,128)} %get-tuple-element.25.base_ref) | copy-start | bytes 36868
  24.7 72.5 %copy-start.3 = (f32[8,128]{1,0:T(8,128)S(1)}, f32[8,128]{1,0:T(8,128)}, u32[]{:S(2)}) copy-start(f32[8,128]{1,0:T(8,128)} %get-tuple-element.26.gain_ref) | copy-start | bytes 12292
  97.2 15.5 %copy-start = (s32[2048,1]{0,1:T(1,128)S(1)}, s32[2048,1]{0,1:T(1,128)}, u32[]{:S(2)}) copy-start(s32[2048,1]{0,1:T(1,128)} %param.18) | copy-start | bytes 24580
  97.2 15.5 %copy-start.2 = (s32[1,2048]{1,0:T(1,128)S(1)}, s32[1,2048]{1,0:T(1,128)}, u32[]{:S(2)}) copy-start(s32[1,2048]{1,0:T(1,128)} %get-tuple-element.22.rank_ref) | copy-start | bytes 24580

commit v5 on v4

--- a/solution.py
+++ b/solution.py
@@ -10,8 +10,9 @@
 EX = TX + 2 * HALO
 EY = 16
 TILES = EX * EY
+NEAR = -(-TILES // 128) * 128
 PLANES = 7
-K = 32
+K = 48
 CAP = 64
 F32, BF16, I32 = jnp.float32, jnp.bfloat16, jnp.int32
 NT = (((1,), (1,)), ((), ()))
@@ -30,24 +31,13 @@
     return high, mid, rest - mid
 
 
+def thirds(x):
+    size = x.shape[0] // 3
+    return x[:size] + x[size : 2 * size] + x[2 * size :]
+
+
 def iota(shape, dim):
     return lax.broadcasted_iota(I32, shape, dim)
-
-
-def distance_rows(xyz):
-    left, right = [], []
-    for comp in xyz:
-        h, m, l = split3(comp)
-        left += [2 * h, 2 * m, 2 * h, 2 * l, 2 * h, 2 * m]
-        right += [h, h, m, h, l, m]
-    norm = xyz[0] * xyz[0] + xyz[1] * xyz[1] + xyz[2] * xyz[2]
-    one = jnp.ones_like(norm)
-    left += list(split3(1.0 - norm)) + [one] * 3
-    right += [one] * 3 + list(split3(-norm))
-    return left, right
-
-
-OWN = slice(HALO, HALO + TX)
 
 
 def pack_kernel(pos_hbm, press_hbm, src_hbm, res_hbm, near_ref, up_ref, down_ref, way_ref, pos, rest, named_v, sems):
@@ -82,16 +72,23 @@
         down_ref[p] = jnp.where(bottom, 0.0, plane[:, :HALO, :])
 
 
+def clear_stage(stage):
+    row = iota((64, L), 0) & 7
+    for place, hot in ((0, 3), (1, 4)):
+        stage[place] = (row == hot).astype(F32)
+
+
 def build_half(xyz, stage):
-    left, right = distance_rows(xyz)
-    for k, row in enumerate(left + right):
-        stage[pl.ds(k if k < len(left) else k - len(left) + K, 8, stride=2 * K), :] = row
-    return stage[...].astype(BF16).reshape(8, 2 * K, L)
-
-
-def store_rows(stage, rows, first, count):
-    for k, row in enumerate(rows):
-        stage[pl.ds(first * K + k, count, stride=K), :] = row
+    norm = xyz[0] * xyz[0] + xyz[1] * xyz[1] + xyz[2] * xyz[2]
+    left = (2 * xyz[0], 2 * xyz[1], 2 * xyz[2], None, 1.0 - norm)
+    right = (xyz[0], xyz[1], xyz[2], -norm)
+    for place, rows in enumerate((left, right)):
+        for k, row in enumerate(rows):
+            if row is not None:
+                stage[place, pl.ds(k, 8, stride=8), :] = row
+    lh, lm, ll = split3(stage[0].reshape(8, 8, L))
+    rh, rm, rl = split3(stage[1].reshape(8, 8, L))
+    return jnp.concatenate([lh, lm, lh, ll, lh, lm, rh, rh, rm, rh, rl, rm], axis=1).astype(BF16)
 
 
 def cube(t):
@@ -103,50 +100,14 @@
     return jnp.sum(acc.T, axis=0, keepdims=True)
 
 
-def side_kernel(yhigh, ylow, out_ref, ext, stage, lr, sems):
-    stage[...] = jnp.zeros_like(stage)
-    ext[...] = jnp.zeros_like(ext)
-    for c in range(3):
-        for x in range(TX):
-            ext[c, x, :HALO, :] = yhigh[c, x]
-            ext[c, x, 8 - HALO :, :] = ylow[c, x]
-    quarter = TX // 4
-
-    def send(i):
-        rows = pl.ds(i * quarter, quarter)
-        return pltpu.make_async_copy(lr.at[rows], out_ref.at[rows], sems.at[i])
-
-    def build(i, _):
-        for e in range(quarter):
-            x = i * quarter + e
-            lr[x] = build_half([ext[c, x] for c in range(3)], stage)
-        send(i).start()
-        return 0
-
-    lax.fori_loop(0, 4, build, 0)
-    for i in range(4):
-        send(i).wait()
-
-
 def prep_kernel(
     contact_ref, owner_ref, pos_ref, vel_ref, mass_ref, own_pos, own_press, own_src, own_res, own_way,
-    rank_ref, base_ref, gain_ref, lr_ref, last_ref, first_ref,
-    stage_a, stage_b, vel, stage, lr, sem,
+    rank_ref, base_ref, gain_ref, last_ref, first_ref,
+    stage, lr, vel,
 ):
     for p, plane in enumerate((own_pos.at[0], own_pos.at[1], own_pos.at[2], own_press, own_src, own_res, own_way)):
         last_ref[p] = plane[TX - HALO :]
         first_ref[p] = plane[:HALO]
-    stage[...] = jnp.zeros_like(stage)
-
-    def build(i, _):
-        for e in range(4):
-            x = i * 4 + e
-            lr[x] = build_half([own_pos[c, x] for c in range(3)], stage)
-        return 0
-
-    lax.fori_loop(0, TX // 4, build, 0)
-    send = pltpu.make_async_copy(lr, lr_ref, sem)
-    send.start()
     owner = owner_ref[...]
     upper = (iota((256, 256), 0) < iota((256, 256), 1)).astype(BF16)
     every = jnp.ones((256, 256), BF16)
@@ -158,26 +119,22 @@
         rank_ref[:, q : q + 256] = jnp.sum(jnp.where(named, before, 0.0), axis=0, keepdims=True).astype(I32)
         carry = carry + dot(hot, every, NN)
     tiles = mass_ref.shape[0]
-    stage_a[...] = jnp.zeros_like(stage_a)
-    stage_b[...] = jnp.zeros_like(stage_b)
+    clear_stage(stage)
     def tiled(ref, c):
         return jnp.concatenate([ref[c : c + 1, t * L : (t + 1) * L] for t in range(tiles)], axis=0)
 
     for c in range(3):
         vel[c] = tiled(vel_ref, c)
-    left, right = distance_rows([tiled(pos_ref, c) for c in range(3)])
-    store_rows(stage_a, left, 0, tiles)
-    store_rows(stage_b, right, 0, tiles)
+    lr[...] = build_half([tiled(pos_ref, c) for c in range(3)], stage)
     gain = 0.1 / mass_ref[...]
     gain_ref[...] = gain
     for t in range(tiles):
-        a = stage_a[t * K : (t + 1) * K, :].astype(BF16)
+        a = lr[t, :K, :]
         total = jnp.zeros((L, L), F32)
         applied = [jnp.zeros((L, L), F32) for _ in range(3)]
         for k in range(4):
             n = contact_ref[k, t]
-            b = stage_b[pl.ds(pl.multiple_of(n * K, K), K), :].astype(BF16)
-            w = cube(dot(a, b, TN))
+            w = cube(dot(a, lr[n, K:, :], TN))
             total = total + w
             for c in range(3):
                 applied[c] = applied[c] + w * vel[c, pl.ds(n, 1), :]
@@ -186,67 +143,68 @@
             own = vel[c, t : t + 1, :]
             contact = (column_sum(applied[c]) - total * own) * (4.0 / 512)
             base_ref[c, t : t + 1, :] = own + gain[t : t + 1, :] * contact
-    send.wait()
 
 
 def fluid_kernel(
-    own_press, own_src, own_res, own_way, ylow, yhigh, xlow, xhigh, lr_own, lr_side, owner_ref, rank_ref, fluid_ref, grain_ref, normal_ref,
+    own_pos, own_press, own_src, own_res, own_way, ylow, yhigh, xlow, xhigh, owner_ref, rank_ref, fluid_ref, grain_ref, normal_ref,
     press_ref, send_ref,
-    ext, near_v, near_s, stage, lr, num_s, deg_s, kept, sem, in_sem,
+    ext, near_v, near_t, near_s, stage, lr, num_s, deg_s, kept, sem,
 ):
     blk, crs = lax.axis_index("blk"), lax.axis_index("crs")
     blks, crss = lax.axis_size("blk"), lax.axis_size("crs")
-    gets = [
-        pltpu.make_async_copy(lr_own, lr.at[OWN, :TY], in_sem.at[0]),
-        pltpu.make_async_copy(lr_side, lr.at[OWN, TY:], in_sem.at[1]),
-    ]
-    for get in gets:
-        get.start()
-    own = (own_press, own_src, own_res, own_way)
-    ext[3:, HALO * EY : (HALO + TX) * EY, :] = jnp.zeros((len(own), TX * EY, L), F32)
-    for x in range(HALO):
-        for p in range(PLANES):
-            ext[p, x * EY : (x + 1) * EY, :] = xlow[p, x]
-            ext[p, (HALO + TX + x) * EY : (HALO + TX + x + 1) * EY, :] = xhigh[p, x]
-    for x in range(TX):
-        r = (HALO + x) * EY
-        for p, plane in enumerate(own, 3):
-            ext[p, r : r + TY, :] = plane[x]
-            ext[p, r + TY : r + TY + HALO, :] = yhigh[p, x]
-            ext[p, r + EY - HALO : r + EY, :] = ylow[p, x]
-    stage[...] = jnp.zeros_like(stage)
+    own = (own_pos.at[0], own_pos.at[1], own_pos.at[2], own_press, own_src, own_res, own_way)
+    ext[:, HALO * EY : (HALO + TX) * EY, :] = jnp.zeros((PLANES, TX * EY, L), F32)
+
+    def fill(planes):
+        for p in planes:
+            for x in range(HALO):
+                ext[p, x * EY : (x + 1) * EY, :] = xlow[p, x]
+                ext[p, (HALO + TX + x) * EY : (HALO + TX + x + 1) * EY, :] = xhigh[p, x]
+            for x in range(TX):
+                r = (HALO + x) * EY
+                ext[p, r : r + TY, :] = own[p][x]
+                ext[p, r + TY : r + TY + HALO, :] = yhigh[p, x]
+                ext[p, r + EY - HALO : r + EY, :] = ylow[p, x]
+
+    fill([6])
 
     def find(ex, _):
         r = pl.multiple_of(ex * EY, EY)
         way = ext[6, pl.ds(r, EY), :].astype(I32)
         dx = lax.shift_right_logical(way * 11, 5)
         dy = way - 3 * dx - 1
-        near_v[pl.ds(r, EY), :] = (ex + dx - 1) * EY + ((iota((EY, L), 0) + dy) & (EY - 1))
+        near_v[pl.ds(r, EY), :] = ((ex + dx - 1) * EY + ((iota((EY, L), 0) + dy) & (EY - 1))).astype(F32)
         return 0
 
     lax.fori_loop(0, EX, find, 0)
-    copy = pltpu.make_async_copy(near_v, near_s, sem)
+    near_v[TILES:, :] = jnp.zeros((NEAR - TILES, L), F32)
+    for t in range(0, NEAR, L):
+        near_t[:, t : t + L] = near_v[t : t + L, :].T[:8].astype(I32)
+    copy = pltpu.make_async_copy(near_t, near_s, sem)
     copy.start()
 
+    fill(range(6))
+    for e in range(4):
+        clear_stage(stage.at[e])
+
     def build(i, _):
-        ex = i + jnp.where(i >= HALO, TX, 0)
-        for half in (0, 8):
+        for e in range(4):
+            ex = 2 * i + e // 2
+            half = e % 2 * 8
             r = pl.multiple_of(ex * EY + half, 8)
-            lr[ex, half : half + 8] = build_half([ext[c, pl.ds(r, 8), :] for c in range(3)], stage)
+            lr[pl.ds(r, 8)] = build_half([ext[c, pl.ds(r, 8), :] for c in range(3)], stage.at[e])
         return 0
 
-    lax.fori_loop(0, 2 * HALO, build, 0)
-    for get in gets:
-        get.wait()
+    lax.fori_loop(0, EX // 2, build, 0)
     copy.wait()
 
     def one_tile(t, with_deg, slot=None):
-        a = lr[lax.shift_right_logical(t, 4), t & (EY - 1), :K, :]
+        a = lr[t, :K, :]
         acc = jnp.zeros((L, L), F32)
         tot = jnp.zeros((L, L), F32)
         for k in range(0, KN, 2):
-            n = [near_s[t, k + e] for e in range(2)]
-            b = jnp.concatenate([lr[lax.shift_right_logical(m, 4), m & (EY - 1), K:, :] for m in n], axis=1)
+            n = [near_s[k + e, t] for e in range(2)]
+            b = jnp.concatenate([lr[m, K:, :] for m in n], axis=1)
             w = cube(dot(a, b, TN))
             for e in range(2):
                 part = w[:, e * L : (e + 1) * L]
@@ -262,7 +220,7 @@
     def kept_tile(t, slot):
         acc = jnp.zeros((L, L), F32)
         for k in range(KN):
-            acc = acc + kept[slot, k] * ext[3, pl.ds(near_s[t, k], 1), :]
+            acc = acc + kept[slot, k] * ext[3, pl.ds(near_s[k, t], 1), :]
         num_s[pl.ds(t, 1), :] = column_sum(acc)
 
     for step in range(ITERS):
@@ -312,7 +270,7 @@
     for x in range(TX):
         press_ref[x] = ext[3, (HALO + x) * EY : (HALO + x) * EY + TY, :]
     press = press_ref[...].reshape(TX * TY, L)
-    parts = jnp.concatenate([s.astype(BF16) for s in split3(press)], axis=1)
+    parts = jnp.concatenate([s.astype(BF16) for s in split3(press)], axis=0)
     total01 = jnp.zeros((64, L), F32)
     total23 = jnp.zeros((64, L), F32)
     chunk = 512
@@ -320,7 +278,7 @@
         cols = slice(q, q + chunk)
         fluid = fluid_ref[:, cols]
         lane = (iota((L, chunk), 0) == (fluid & (L - 1))).astype(F32).astype(BF16)
-        found = dot(parts, jnp.concatenate([lane] * 3, axis=0), NN)
+        found = thirds(dot(parts, lane, NN))
         tile = iota((TX * TY, chunk), 0) == lax.shift_right_logical(fluid, 7)
         at = jnp.sum(jnp.where(tile, found, 0.0), axis=0, keepdims=True)
         owned = iota((64, chunk), 0) == owner_ref[:, cols]
@@ -360,20 +318,20 @@
         new.append(base_ref[c] + gain_ref[...] * coupling)
         for g in range(8):
             new_ref[c : c + 1, g * L : (g + 1) * L] = new[c][g : g + 1]
-    parts = jnp.concatenate([s.astype(BF16) for s in split3(jnp.concatenate(new, axis=0))], axis=1)
-    found = dot(parts, jnp.concatenate([lane] * 3, axis=0), NN)
+    parts = jnp.concatenate([s for s in split3(jnp.concatenate(new, axis=0))], axis=0).astype(BF16)
+    found = thirds(dot(parts, lane, NN))
     for c in range(3):
         back_ref[c : c + 1, :] = jnp.sum(jnp.where(tile, found[c * 8 : c * 8 + 8], 0.0), axis=0, keepdims=True)
 
 
 def pick_kernel(got_ref, owner_ref, rank_ref, out_ref):
     blocks = jnp.concatenate([got_ref[:, c * CAP : (c + 1) * CAP] for c in range(3)], axis=0)
-    parts = [s.astype(BF16) for s in split3(blocks)]
+    parts = jnp.concatenate([s.astype(BF16) for s in split3(blocks)], axis=0)
     chunk = 512
     for q in range(0, owner_ref.shape[1], chunk):
         cols = slice(q, q + chunk)
         slot = (iota((CAP, chunk), 0) == rank_ref[:, cols]).astype(F32).astype(BF16)
-        found = dot(parts[0], slot, NN) + dot(parts[1], slot, NN) + dot(parts[2], slot, NN)
+        found = thirds(dot(parts, slot, NN))
         owned = iota((64, chunk), 0) == owner_ref[:, cols]
         for c in range(3):
             out_ref[c : c + 1, cols] = jnp.sum(jnp.where(owned, found[c * 64 : (c + 1) * 64], 0.0), axis=0, keepdims=True)
@@ -405,7 +363,7 @@
     fluid = pair_fluid.reshape(1, pairs)
     grain = pair_grain.reshape(1, pairs)
     semaphore = pltpu.SemaphoreType.DMA
-    params = pltpu.CompilerParams(vmem_limit_bytes=62 << 20)
+    params = pltpu.CompilerParams(vmem_limit_bytes=63 << 20)
     rim_y, rim_x = shape(PLANES, TX, HALO, L), shape(PLANES, HALO, TY, L)
     up, down, way = pl.pallas_call(
         pack_kernel,
@@ -421,14 +379,12 @@
     ylow = lax.ppermute(up, "crs", forward)
     yhigh = lax.ppermute(down, "crs", backward)
     grain_tiles = grain_mass.shape[0] // L
-    half = shape(TX, 8, 2 * K, L, dtype=BF16)
-    half_scratch = [pltpu.VMEM((8 * 2 * K, L), F32), pltpu.VMEM((TX, 8, 2 * K, L), BF16)]
-    rank, base, gain, lr_own, last, first = pl.pallas_call(
+    rank, base, gain, last, first = pl.pallas_call(
         prep_kernel,
-        out_shape=(shape(1, pairs, dtype=I32), shape(3, grain_tiles, L), shape(grain_tiles, L), half, rim_x, rim_x),
+        out_shape=(shape(1, pairs, dtype=I32), shape(3, grain_tiles, L), shape(grain_tiles, L), rim_x, rim_x),
         in_specs=[SMEM] + [VMEM] * 9,
-        out_specs=(VMEM, VMEM, VMEM, HBM, VMEM, VMEM),
-        scratch_shapes=[pltpu.VMEM((grain_tiles * K, L), F32)] * 2 + [pltpu.VMEM((3, grain_tiles, L), F32)] + half_scratch + [semaphore],
+        out_specs=(VMEM,) * 5,
+        scratch_shapes=[pltpu.VMEM((2, 64, L), F32), pltpu.VMEM((grain_tiles, 2 * K, L), BF16)] + [pltpu.VMEM((3, grain_tiles, L), F32)],
         compiler_params=params,
         cost_estimate=cost(10**9, 10**6),
         name="prep",
@@ -443,38 +399,27 @@
     xlow = lax.ppermute(jnp.where(here == count - 1, 0.0, wide(last, slice(-HALO, None))), "blk", forward)
     xhigh = lax.ppermute(jnp.where(here == 0, 0.0, wide(first, slice(0, HALO))), "blk", backward)
 
-    lr_side = pl.pallas_call(
-        side_kernel,
-        out_shape=half,
-        in_specs=[VMEM] * 2,
-        out_specs=HBM,
-        scratch_shapes=[pltpu.VMEM((3, TX, 8, L), F32), *half_scratch, semaphore((4,))],
-        compiler_params=params,
-        cost_estimate=cost(10**9, 10**6),
-        name="side",
-    )(yhigh, ylow)
-
     press, send = pl.pallas_call(
         fluid_kernel,
         out_shape=(shape(TX, TY, L), shape(64, 2, L)),
-        in_specs=[VMEM] * 8 + [HBM] * 2 + [VMEM] * 5,
+        in_specs=[VMEM] * 14,
         out_specs=(VMEM,) * 2,
         scratch_shapes=[
             pltpu.VMEM((PLANES, TILES, L), F32),
-            pltpu.VMEM((TILES, L), I32),
-            pltpu.SMEM((TILES, L), I32),
-            pltpu.VMEM((8 * 2 * K, L), F32),
-            pltpu.VMEM((EX, EY, 2 * K, L), BF16),
+            pltpu.VMEM((NEAR, L), F32),
+            pltpu.VMEM((8, NEAR), I32),
+            pltpu.SMEM((8, NEAR), I32),
+            pltpu.VMEM((4, 2, 64, L), F32),
+            pltpu.VMEM((TILES, 2 * K, L), BF16),
             pltpu.VMEM((TILES, L), F32),
             pltpu.VMEM((TILES, L), F32),
             pltpu.VMEM((TX * TY, KN, L, L), F32),
             semaphore,
-            semaphore((2,)),
         ],
-        compiler_params=pltpu.CompilerParams(vmem_limit_bytes=62 << 20),
+        compiler_params=pltpu.CompilerParams(vmem_limit_bytes=63 << 20),
         cost_estimate=cost(10**10, 10**7),
         name="fluid",
-    )(pressure_start, source, resist, way, ylow, yhigh, xlow, xhigh, lr_own, lr_side, owner, rank, fluid, grain, pair_normal)
+    )(positions, pressure_start, source, resist, way, ylow, yhigh, xlow, xhigh, owner, rank, fluid, grain, pair_normal)
 
     got = lax.all_to_all(send, "blk", 0, 0, tiled=True)
     got = got.reshape(64, 4, CAP).swapaxes(0, 1).reshape(4, 64 * CAP)

time: 115 us -> 113 us (0.983)
  Pallas kernels: 65.8 us -> 58.3 us
  waiting for transfers between devices: 2.38 us -> 7.42 us
  local copies, waits for them, and re-layouts: 1.4 us -> 3.17 us
    pallas_call x1 -> x0, Pallas kernels: 3.85 us -> none  [on_device(): pl.pallas_call(side_kernel, out_shape=half, in_specs=[VMEM] * 2, out_spec...]
    ppermute x1, starting transfers between devices: 0.01 us -> 3.1 us  [on_device(): lax.ppermute(jnp.where(here == 0, 0.0, wide(first, slice(0, HALO))), 'blk...]
    pallas_call x1, Pallas kernels: 6.01 us -> 3.01 us  [on_device(): pl.pallas_call(prep_kernel, out_shape=(shape(1, pairs, dtype=I32), shape(...]
    ppermute x1, waiting for transfers between devices: 0.01 us -> 2.97 us  [on_device(): lax.ppermute(jnp.where(here == count - 1, 0.0, wide(last, slice(-HALO, No...]
    ppermute x1, starting transfers between devices: 3.46 us -> 1.26 us  [on_device(): lax.ppermute(jnp.where(here == count - 1, 0.0, wide(last, slice(-HALO, No...]
    ppermute x1, starting transfers between devices: 0.01 us -> 2.2 us  [on_device(): ylow = lax.ppermute(up, 'crs', forward)]
    ppermute x1, starting transfers between devices: 3.64 us -> 1.53 us  [on_device(): yhigh = lax.ppermute(down, 'crs', backward)]
    ppermute x1, waiting for transfers between devices: 0.94 us -> 3 us  [on_device(): lax.ppermute(jnp.where(here == 0, 0.0, wide(first, slice(0, HALO))), 'blk...]
  transfers between devices with their start and end apart: 4 -> 4, of which waited for: 2 -> 4; matrix products, arithmetic and copies ran while one was open for 0% -> 0% of each run, Pallas kernels for 9% -> 3%
where the time goes in v5:
time: 113 us
  Pallas kernels  58.3 us (52%)
  blocking collectives  34.8 us (31%)
  starting transfers between devices  8.09 us (7%)
  waiting for transfers between devices  7.42 us (7%)
  local copies, waits for them, and re-layouts  3.17 us (3%)
    pallas_call x1, Pallas kernels, on_device(): pl.pallas_call(fluid_kernel, out_shape=(shape(TX, TY, L), shape(64, 2, L)...  49.8 us
    all_to_all x1, blocking collectives, on_device(): got = lax.all_to_all(send, 'blk', 0, 0, tiled=True)  21.2 us
    all_to_all x1, blocking collectives, on_device(): seen = lax.all_to_all(back, 'blk', 0, 0, tiled=True)  13.6 us
    ppermute x1, starting transfers between devices, on_device(): lax.ppermute(jnp.where(here == 0, 0.0, wide(first, slice(0, HALO))), 'blk...  3.1 us
    pallas_call x1, Pallas kernels, on_device(): pl.pallas_call(prep_kernel, out_shape=(shape(1, pairs, dtype=I32), shape(...  3.01 us
    ppermute x1, waiting for transfers between devices, on_device(): lax.ppermute(jnp.where(here == 0, 0.0, wide(first, slice(0, HALO))), 'blk...  3 us
    ppermute x1, waiting for transfers between devices, on_device(): lax.ppermute(jnp.where(here == count - 1, 0.0, wide(last, slice(-HALO, No...  2.97 us
    pallas_call x1, Pallas kernels, on_device(): pl.pallas_call(pack_kernel, out_shape=(rim_y, rim_y, shape(TX, TY, L)), i...  2.71 us
  transfers between devices with their start and end apart: 4, of which 4 were waited for; matrix products, arithmetic and copies ran while one was open for 0% of the time, Pallas kernels for 3%

profile of v5, /device:TPU:1, one launch (start us, length us, event | category | flops | bytes accessed | tf_op | source)
XLA Modules:
  0.0 112.7 jit_solution(4274828997540686537)
XLA Ops:
  0.6 2.7 %pack.1 = (f32[7,16,3,128]{3,2,1,0:T(4,128)}, f32[7,16,3,128]{3,2,1,0:T(4,128)}, f32[16,8,128]{2,1,0:T(8,128)}) custom-call(f32[3,16,8,128]{3,2,1,0:T(8,128)} %own_pos.3, f32[16,8,128]{2,1,0:T(8,128)} %own_press.3, f32[16,8,128]{2,1,0:T(8,128)} %own_src.3, f32[16,8,128]{2,1,0:T(8,128)} %own_res.3, s32[6,8,16]{2,1,0:T(8,128)} %bitcast.21), custom_call_target="tpu_custom_call" | custom-call | flops 1000000 | bytes 1000000 | tf_op jit(solution)/shard_map/pack/pallas_call | solution.py:368
  3.4 2.2 %collective-permute-start = (f32[7,16,3,128]{3,2,1,0:T(4,128)}, f32[7,16,3,128]{3,2,1,0:T(4,128)S(1)}, u32[]{:S(2)}, u32[]{:S(2)}) collective-permute-start(f32[7,16,3,128]{3,2,1,0:T(4,128)} %get-tuple-element.16), channel_id=1, source_target_pairs={{0,1},{1,2},{2,3},{3,0},{4,5},{5,6},{6,7},{7,4},{8,9},{9,10},{10,1... | collective-permute-start | bytes 516104 | tf_op jit(solution)/shard_map/ppermute | solution.py:379
  5.6 1.5 %collective-permute-start.1 = (f32[7,16,3,128]{3,2,1,0:T(4,128)}, f32[7,16,3,128]{3,2,1,0:T(4,128)S(1)}, u32[]{:S(2)}, u32[]{:S(2)}) collective-permute-start(f32[7,16,3,128]{3,2,1,0:T(4,128)} %get-tuple-element.17), channel_id=1, source_target_pairs={{1,0},{2,1},{3,2},{0,3},{5,4},{6,5},{7,6},{4,7},{9,8},{10,9},{11,1... | collective-permute-start | bytes 516104 | tf_op jit(solution)/shard_map/ppermute | solution.py:380
  7.1 0.1 pad.6.clone
  7.2 3.0 %prep.1 = (s32[1,2048]{1,0:T(1,128)}, f32[3,8,128]{2,1,0:T(8,128)}, f32[8,128]{1,0:T(8,128)}, f32[7,3,8,128]{3,2,1,0:T(8,128)}, f32[7,3,8,128]{3,2,1,0:T(8,128)}) custom-call(s32[4,8]{1,0:T(4,128)} %bitcast.25, s32[1,2048]{1,0:T(1,128)} %bitcast.16, f32[3,1024]{1,0:T(4,128)} %pos_ref.1, f32[3,1024]{1,0:T(4,128)} %vel_ref.1, f32[8,128]{1,0:T(8,128)} %bitcast.24, ...), custom_call_target="tpu_custom_call" | custom-call | flops 1000000000 | bytes 1000000 | tf_op jit(solution)/shard_map/prep/pallas_call | solution.py:382
  10.2 0.4 collective-permute-done.ylow
  10.6 0.0 copy-start.6
  10.6 0.0 copy-start.4
  10.6 0.0 copy-start.5
  10.7 1.0 collective-permute-done.1.yhigh
  11.7 0.0 copy-start.7
  11.7 0.0 copy-done.4
  11.7 0.0 copy-done.5
  11.7 0.1 maximum_select_fusion.1
  11.8 0.0 copy-done.6
  11.8 0.5 copy-done.7
  12.3 3.1 %collective-permute-start.3 = (f32[7,3,16,128]{3,2,1,0:T(8,128)S(1)}, f32[7,3,16,128]{3,2,1,0:T(8,128)S(1)}, u32[]{:S(2)}, u32[]{:S(2)}) collective-permute-start(f32[7,3,16,128]{3,2,1,0:T(8,128)S(1)} %get-tuple-element.31), channel_id=1, source_target_pairs={{4,0},{8,4},{12,8},{16,12},{20,16},{24,20},{28,24},{32,28},{36,32}... | collective-permute-start | bytes 516104 | tf_op jit(solution)/shard_map/ppermute | solution.py:400
  15.4 1.3 %collective-permute-start.2 = (f32[7,3,16,128]{3,2,1,0:T(8,128)S(1)}, f32[7,3,16,128]{3,2,1,0:T(8,128)S(1)}, u32[]{:S(2)}, u32[]{:S(2)}) collective-permute-start(f32[7,3,16,128]{3,2,1,0:T(8,128)S(1)} %get-tuple-element.32), channel_id=1, source_target_pairs={{0,4},{4,8},{8,12},{12,16},{16,20},{20,24},{24,28},{28,32},{32,36}... | collective-permute-start | bytes 516104 | tf_op jit(solution)/shard_map/ppermute | solution.py:399
  16.7 3.0 %collective-permute-done.3.xhigh = f32[7,3,16,128]{3,2,1,0:T(8,128)S(1)} collective-permute-done((f32[7,3,16,128]{3,2,1,0:T(8,128)S(1)}, f32[7,3,16,128]{3,2,1,0:T(8,128)S(1)}, u32[]{:S(2)}, u32[]{:S(2)}) %collective-permute-start.3) | collective-permute-done | bytes 172064 | tf_op jit(solution)/shard_map/ppermute | solution.py:400
  19.7 0.0 copy-start.8
  19.7 3.0 %collective-permute-done.2.xlow = f32[7,3,16,128]{3,2,1,0:T(8,128)S(1)} collective-permute-done((f32[7,3,16,128]{3,2,1,0:T(8,128)S(1)}, f32[7,3,16,128]{3,2,1,0:T(8,128)S(1)}, u32[]{:S(2)}, u32[]{:S(2)}) %collective-permute-start.2) | collective-permute-done | bytes 172064 | tf_op jit(solution)/shard_map/ppermute | solution.py:399
  22.7 0.0 copy-start.9
  22.7 0.0 copy-done.8
  22.7 0.7 copy-done.9
  23.3 49.8 %fluid.1 = (f32[16,8,128]{2,1,0:T(8,128)}, f32[64,2,128]{2,1,0:T(2,128)}) custom-call(f32[3,16,8,128]{3,2,1,0:T(8,128)} %own_pos.3, f32[16,8,128]{2,1,0:T(8,128)} %own_press.3, f32[16,8,128]{2,1,0:T(8,128)} %own_src.3, f32[16,8,128]{2,1,0:T(8,128)} %own_res.3, f32[16,8,128]{2,1,0:T(8,128)} %get-tuple-element.15.own_way, f32[7,16,3,128]{3,2,1,0:T(4,128)} %copy-done.6, ...), custom_call_target="tpu_custom_call" | custom-call | flops 10000000000 | bytes 10000000 | tf_op jit(solution)/shard_map/fluid/pallas_call | solution.py:402
  73.2 21.2 %all_to_all.16 = f32[64,2,128]{2,1,0:T(2,128)S(1)} all-to-all(f32[64,2,128]{2,1,0:T(2,128)} %get-tuple-element.22), channel_id=1, replica_groups=mesh['blk'=64,'crs'=4] {'blk'}, dimensions={0} | all-to-all | bytes 131072 | tf_op jit(solution)/shard_map/all_to_all | solution.py:424
  94.4 0.1 reshape.35
  94.6 0.0 copy-start.1
  94.6 0.0 copy-start.3
  94.6 0.1 reshape.36.got_ref
  94.7 0.6 copy-done.1
  95.3 0.0 copy-done.3
  95.3 1.3 %grain.1 = (f32[3,1024]{1,0:T(4,128)}, f32[3,4096]{1,0:T(4,128)S(1)}) custom-call(f32[4,4096]{1,0:T(4,128)S(1)} %reshape.36.got_ref, f32[3,8,128]{2,1,0:T(8,128)S(1)} %copy-done.1, f32[8,128]{1,0:T(8,128)S(1)} %copy-done.3), custom_call_target="tpu_custom_call" | custom-call | flops 1000000000 | bytes 1000000 | tf_op jit(solution)/shard_map/grain/pallas_call | solution.py:426
  96.6 0.1 reshape.37
  96.7 0.1 copy.22
  96.8 0.1 copy.23
  96.9 13.6 %all_to_all.17 = f32[64,1,192]{2,1,0:T(1,128)S(1)} all-to-all(f32[64,1,192]{2,1,0:T(1,128)S(1)} %copy.23), channel_id=1, replica_groups=mesh['blk'=64,'crs'=4] {'blk'}, dimensions={0} | all-to-all | bytes 98304 | tf_op jit(solution)/shard_map/all_to_all | solution.py:436
  110.5 0.0 copy-start
  110.6 0.0 copy-start.2
  110.6 0.7 copy-done
  111.2 0.0 copy-done.2
  111.3 1.4 %pick.1 = f32[3,2048]{1,0:T(4,128)} custom-call(f32[64,192]{1,0:T(8,128)S(1)} %bitcast.15, s32[1,2048]{1,0:T(1,128)S(1)} %bitcast.18, s32[1,2048]{1,0:T(1,128)S(1)} %copy-done.2), custom_call_target="tpu_custom_call" | custom-call | flops 1000000000 | bytes 1000000 | tf_op jit(solution)/shard_map/pick/pallas_call | solution.py:437
  (5 shorter events, 0.0 us)
Async XLA Ops:
  3.4 7.3 %collective-permute-start = (f32[7,16,3,128]{3,2,1,0:T(4,128)}, f32[7,16,3,128]{3,2,1,0:T(4,128)S(1)}, u32[]{:S(2)}, u32[]{:S(2)}) collective-permute-start(f32[7,16,3,128]{3,2,1,0:T(4,128)} %get-tuple-element.16), channel_id=1, source_target_pairs={{0,1},{1,2},{2,3},{3,0},{4,5},{5,6},{6,7},{7,4},{8,9},{9,10},{10,1... | collective-permute-start | bytes 516104 | tf_op jit(solution)/shard_map/ppermute | solution.py:379
  5.6 6.1 %collective-permute-start.1 = (f32[7,16,3,128]{3,2,1,0:T(4,128)}, f32[7,16,3,128]{3,2,1,0:T(4,128)S(1)}, u32[]{:S(2)}, u32[]{:S(2)}) collective-permute-start(f32[7,16,3,128]{3,2,1,0:T(4,128)} %get-tuple-element.17), channel_id=1, source_target_pairs={{1,0},{2,1},{3,2},{0,3},{5,4},{6,5},{7,6},{4,7},{9,8},{10,9},{11,1... | collective-permute-start | bytes 516104 | tf_op jit(solution)/shard_map/ppermute | solution.py:380
  10.6 1.2 %copy-start.6 = (f32[7,16,3,128]{3,2,1,0:T(4,128)}, f32[7,16,3,128]{3,2,1,0:T(4,128)S(1)}, u32[]{:S(2)}) copy-start(f32[7,16,3,128]{3,2,1,0:T(4,128)S(1)} %collective-permute-done.ylow) | copy-start | bytes 516100
  10.6 1.0 copy-start.4
  10.6 1.0 copy-start.5
  11.7 0.7 copy-start.7
  12.3 7.4 %collective-permute-start.3 = (f32[7,3,16,128]{3,2,1,0:T(8,128)S(1)}, f32[7,3,16,128]{3,2,1,0:T(8,128)S(1)}, u32[]{:S(2)}, u32[]{:S(2)}) collective-permute-start(f32[7,3,16,128]{3,2,1,0:T(8,128)S(1)} %get-tuple-element.31), channel_id=1, source_target_pairs={{4,0},{8,4},{12,8},{16,12},{20,16},{24,20},{28,24},{32,28},{36,32}... | collective-permute-start | bytes 516104 | tf_op jit(solution)/shard_map/ppermute | solution.py:400
  15.4 7.2 %collective-permute-start.2 = (f32[7,3,16,128]{3,2,1,0:T(8,128)S(1)}, f32[7,3,16,128]{3,2,1,0:T(8,128)S(1)}, u32[]{:S(2)}, u32[]{:S(2)}) collective-permute-start(f32[7,3,16,128]{3,2,1,0:T(8,128)S(1)} %get-tuple-element.32), channel_id=1, source_target_pairs={{0,4},{4,8},{8,12},{12,16},{16,20},{20,24},{24,28},{28,32},{32,36}... | collective-permute-start | bytes 516104 | tf_op jit(solution)/shard_map/ppermute | solution.py:399
  19.7 3.0 %copy-start.8 = (f32[7,3,16,128]{3,2,1,0:T(8,128)}, f32[7,3,16,128]{3,2,1,0:T(8,128)S(1)}, u32[]{:S(2)}) copy-start(f32[7,3,16,128]{3,2,1,0:T(8,128)S(1)} %collective-permute-done.3.xhigh) | copy-start | bytes 516100
  22.7 0.7 copy-start.9
  94.6 0.7 copy-start.1
  94.6 0.7 copy-start.3
  110.5 0.7 copy-start
  110.6 0.7 copy-start.2
